TPU v7x, 32 devices: a whole 2x2x4 slice. The times are simulated.
32 devices in a mesh: groups: 2 (over y), scen: 8 (over z, x), lane: 1, dep: 2 (over core).
Axes of the slice: x: 2, y: 2, z: 4, core: 2. Of those that a mesh axis runs over, the one named last changes fastest.
Arguments:
- tiles: bfloat16 [32, 1, 2, 8, 128, 128], P(('groups', 'scen'), 'lane', 'dep'), parts along dimension 0, may hold values from -0.5 to 0.5
- row_index: int32 [32, 1, 2, 8], P(('groups', 'scen'), 'lane', 'dep'), parts along dimension 0, may hold values from 0 to 15
- col_index: int32 [32, 1, 2, 8], P(('groups', 'scen'), 'lane', 'dep'), parts along dimension 0, may hold values from 0 to 15
- tile_count: int32 [32, 1, 2], P(('groups', 'scen'), 'lane', 'dep'), parts along dimension 0, may hold values from 4 to 8, as said below
- demand: float32 [32, 2048], P(('groups', 'scen'), 'lane'), parts along dimension 0, may hold values from -12 to 12
- root_cost: float32 [8192], P(('groups', 'dep')), parts along dimension 0, may hold values from -1 to 0.5
- branch_cost: float32 [32, 4096], P(('groups', 'scen'), 'dep'), parts along dimension 0, may hold values from -0.8 to 0.4
- dispatch_cost: float32 [32, 4096], P(('groups', 'scen'), 'dep'), parts along dimension 0, may hold values from -0.6 to 0.3
- branch_of: int32 [32], P(('groups', 'scen')), parts along dimension 0, may hold values from 0 to 7, as said below
Outputs:
- fleet_plan: float32 [32, 4096], P(('groups', 'scen'), 'dep'), parts along dimension 0
- assign_plan: float32 [32, 4096], P(('groups', 'scen'), 'dep'), parts along dimension 0
- dispatch_plan: float32 [32, 4096], P(('groups', 'scen'), 'dep'), parts along dimension 0
- cover_dual: float32 [32, 2048], P(('groups', 'scen'), 'lane'), parts along dimension 0
- fleet_price: float32 [32, 4096], P(('groups', 'scen'), 'dep'), parts along dimension 0
- assign_price: float32 [32, 4096], P(('groups', 'scen'), 'dep'), parts along dimension 0
There are 2 independent parts, one for each index of `groups`. A program takes and returns all parts, laid end to end along the dimension named above; each array names one. Nothing has to cross between parts.
Inputs may be any that keep to these rules, and one draw needn't show every extreme that they name: `tile_count`: at least half of the 8 slots of each block are live, and some block has all of them live. `branch_of`: every branch holds exactly 2 scenarios.
All inputs are finite; a program needn't handle non-finite values.
Results may differ from a plain program's by a relative error of at most 0.0022.
Values may be sent and summed in bfloat16 or wider, within the bound.
A program may use at most 64 MiB of HBM per device.

v0:
```python
import functools

import jax
import jax.numpy as jnp
from jax import lax
from jax.experimental import pallas as pl
from jax.experimental.pallas import tpu as pltpu
from jax.sharding import PartitionSpec as P

BRANCHES = 8
ITERS = 2
STEPS = 4


step_scale = 0.2
penalty = 1.0
epsilon = 1e-06


def reweigh(weight_ratio, totals, col_total, lane_total):
    primal_rate = totals[:, 0] / (3.0 * col_total)
    dual_rate = totals[:, 1] / (lane_total + 2.0 * col_total)
    target = jnp.sqrt((primal_rate + epsilon) / (dual_rate + epsilon))
    return jnp.sqrt(weight_ratio * target)


def pick_rows(source, places):
    return source[places]


def local(
    tiles,
    row_index,
    col_index,
    tile_count,
    demand,
    root_cost,
    branch_cost,
    dispatch_cost,
    branch_of,
):
    highest = lax.Precision.HIGHEST
    scen_here = tiles.shape[0]
    slots = tiles.shape[3]
    tile_size = tiles.shape[5]
    blocks = tiles.reshape(scen_here, slots, tile_size, tile_size)
    row_ids = row_index.reshape(scen_here, slots)
    col_ids = col_index.reshape(scen_here, slots)
    live_count = tile_count.reshape(scen_here)
    width = root_cost.shape[0]
    lane_rows = demand.shape[1]
    col_blocks = width // tile_size
    row_blocks = lane_rows // tile_size
    lane_count = lax.axis_size("lane")
    col_total = float(width * lax.axis_size("dep"))
    lane_total = float(lane_rows * lane_count)
    slot_iota = lax.broadcasted_iota(jnp.int32, (scen_here, slots), 1)
    live_mask = (slot_iota < live_count[:, None]).astype(jnp.float32)
    row_table = (row_ids[:, :, None] == jnp.arange(row_blocks, dtype=jnp.int32)).astype(
        jnp.float32
    ) * live_mask[:, :, None]
    col_table = (col_ids[:, :, None] == jnp.arange(col_blocks, dtype=jnp.int32)).astype(
        jnp.float32
    ) * live_mask[:, :, None]
    single_copy = (lax.axis_index("lane") == 0).astype(jnp.float32)
    dep_first = (lax.axis_index("dep") == 0).astype(jnp.float32)
    zeros_cols = jnp.zeros((scen_here, width), jnp.float32)
    fleet_plan = zeros_cols
    assign_plan = zeros_cols
    dispatch_plan = zeros_cols
    fleet_dual = zeros_cols
    assign_dual = zeros_cols
    fleet_price = zeros_cols
    assign_price = zeros_cols
    assign_mean = zeros_cols
    fleet_mean = jnp.zeros((width,), jnp.float32)
    cover_dual = jnp.zeros((scen_here, lane_rows), jnp.float32)
    weight_ratio = jnp.ones((scen_here,), jnp.float32)
    branch_table = (branch_of[:, None] == jnp.arange(BRANCHES, dtype=jnp.int32)).astype(jnp.float32)
    total_scen = scen_here * lax.axis_size("scen")
    per_branch = total_scen // BRANCHES
    for hedge_round in range(ITERS):
        penalty_now = 0.0 if hedge_round == 0 else penalty
        for inner_step in range(STEPS):
            closing = hedge_round == ITERS - 1 and inner_step == STEPS - 1
            picked = jax.vmap(pick_rows)(
                cover_dual.astype(jnp.bfloat16).reshape(scen_here, row_blocks, tile_size), row_ids
            )
            products = jnp.einsum(
                "snij,sni->snj", blocks, picked, preferred_element_type=jnp.float32
            )
            partial_value = jnp.einsum(
                "snc,snj->scj", col_table, products, precision=highest
            ).reshape(scen_here, width)
            pulled = lax.psum(partial_value, "lane")
            primal_step = step_scale / weight_ratio[:, None]
            dual_step = step_scale * weight_ratio[:, None]
            fleet_new = jnp.maximum(
                0.0,
                fleet_plan
                - primal_step
                * (
                    root_cost[None, :]
                    + fleet_price
                    + penalty_now * (fleet_plan - fleet_mean[None, :])
                    - fleet_dual
                ),
            )
            assign_new = jnp.maximum(
                0.0,
                assign_plan
                - primal_step
                * (
                    branch_cost
                    + assign_price
                    + penalty_now * (assign_plan - assign_mean)
                    + fleet_dual
                    - assign_dual
                ),
            )
            dispatch_new = jnp.maximum(
                0.0, dispatch_plan - primal_step * (dispatch_cost + assign_dual - pulled)
            )
            fleet_ext = 2.0 * fleet_new - fleet_plan
            assign_ext = 2.0 * assign_new - assign_plan
            dispatch_ext = 2.0 * dispatch_new - dispatch_plan
            assign_dual_new = jnp.maximum(
                0.0, assign_dual + dual_step * (dispatch_ext - assign_ext)
            )
            fleet_dual_new = jnp.maximum(0.0, fleet_dual + dual_step * (assign_ext - fleet_ext))
            extrap_bf = dispatch_ext.astype(jnp.bfloat16)
            forward_picked = jax.vmap(pick_rows)(
                extrap_bf.reshape(scen_here, col_blocks, tile_size), col_ids
            )
            forward_products = jnp.einsum(
                "snij,snj->sni", blocks, forward_picked, preferred_element_type=jnp.float32
            )
            load_part = jnp.einsum(
                "snr,sni->sri", row_table, forward_products, precision=highest
            ).reshape(scen_here, lane_rows)
            primal_moves = single_copy * jnp.sum(
                (fleet_new - fleet_plan) ** 2
                + (assign_new - assign_plan) ** 2
                + (dispatch_new - dispatch_plan) ** 2,
                axis=1,
            )
            pair_moves = single_copy * jnp.sum(
                (assign_dual_new - assign_dual) ** 2 + (fleet_dual_new - fleet_dual) ** 2, axis=1
            )
            lane_load = lax.psum(load_part, "dep")
            cover_new = jnp.maximum(0.0, cover_dual + dual_step * (demand - lane_load))
            cover_moves = jnp.sum((cover_new - cover_dual) ** 2, axis=1)
            if not closing:
                totals = lax.psum(
                    jnp.stack([primal_moves, pair_moves + dep_first * cover_moves], axis=1),
                    ("lane", "dep"),
                )
                weight_ratio = reweigh(weight_ratio, totals, col_total, lane_total)
            fleet_plan, assign_plan, dispatch_plan = (fleet_new, assign_new, dispatch_new)
            fleet_dual, assign_dual, cover_dual = (fleet_dual_new, assign_dual_new, cover_new)
        root_local = jnp.sum(fleet_plan, axis=0)
        branch_local = jnp.dot(branch_table.T, assign_plan, precision=highest)
        root_total, branch_total = lax.psum((root_local, branch_local), "scen")
        fleet_mean = root_total / total_scen
        branch_means = branch_total / per_branch
        assign_mean = jnp.dot(branch_table, branch_means, precision=highest)
        fleet_price = fleet_price + penalty * (fleet_plan - fleet_mean[None, :])
        assign_price = assign_price + penalty * (assign_plan - assign_mean)
    return (fleet_plan, assign_plan, dispatch_plan, cover_dual, fleet_price, assign_price)


MESH = pl.DeviceIdType.MESH


def dot(a, b):
    return jnp.dot(a, b, preferred_element_type=jnp.float32)


def dot_t(a, b):
    return lax.dot_general(a, b, (((1,), (1,)), ((), ())), preferred_element_type=jnp.float32)


def total(x):
    return jnp.sum(x, axis=(0, 1), keepdims=True)


def fused(
    n_scen,
    tiles,
    row_index,
    col_index,
    tile_count,
    demand,
    root_cost,
    branch_cost,
    dispatch_cost,
    branch_of,
    fleet_out,
    assign_out,
    dispatch_out,
    cover_out,
    fleet_price_out,
    assign_price_out,
    blocks,
    costs_out,
    costs,
    ids_out,
    ids_in,
    cover_rows,
    dispatch_rows,
    gather_out,
    gather_in,
    reply_out,
    reply_in,
    early_out,
    early_in,
    late_out,
    late_in,
    local_sem,
    pair_send,
    pair_recv,
    group_send,
    group_recv,
):
    here = lax.axis_index("dep")
    other = 1 - here
    chip = lax.axis_index("scen")
    me = 2 * chip + here
    members = 2 * n_scen
    slots = tiles.shape[1]
    tile = tiles.shape[2]
    lane_rows = demand.shape[1]
    width = branch_cost.shape[1]
    row_blocks = lane_rows // tile
    col_blocks = width // tile
    col_total = float(2 * width)
    lane_total = float(lane_rows)
    total_scen = float(members)
    per_branch = float(members // BRANCHES)

    def member(k):
        to = lax.rem(me + k, members)
        return to, {"scen": to // 2, "dep": lax.rem(to, 2)}

    barrier = pltpu.get_barrier_semaphore()
    for k in range(1, members):
        _, device = member(k)
        pl.semaphore_signal(barrier, inc=1, device_id=device, device_id_type=MESH)

    own_tiles = pltpu.make_async_copy(tiles.at[here], blocks.at[0], local_sem)
    own_tiles.start()

    def put_rows(own, far, source):
        for c in range(source.shape[1] // tile):
            row_0 = source[0:1, c * tile : (c + 1) * tile]
            row_1 = source[1:2, c * tile : (c + 1) * tile]
            own[c : c + 1, :] = jnp.where(here == 0, row_0, row_1)
            if far is not None:
                far[c : c + 1, :] = jnp.where(here == 0, row_1, row_0)

    put_rows(costs.at[0, 0], costs_out.at[0], branch_cost)
    put_rows(costs.at[0, 1], costs_out.at[1], dispatch_cost)
    costs_out[2] = root_cost[...]
    costs[0, 2] = root_cost[...]
    for j in range(slots):
        ids_out[j] = row_index[other, 0, 0, j]
        ids_out[slots + j] = col_index[other, 0, 0, j]
    ids_out[2 * slots] = tile_count[other, 0, 0]

    def pair(source, target, at):
        return pltpu.make_async_remote_copy(
            src_ref=source,
            dst_ref=target,
            send_sem=pair_send.at[at],
            recv_sem=pair_recv.at[at],
            device_id={"dep": other},
            device_id_type=MESH,
        )

    pl.semaphore_wait(barrier, members - 1)
    ids_copy = pair(ids_out, ids_in, 0)
    ids_copy.start()
    costs_copy = pair(costs_out, costs.at[1], 1)
    costs_copy.start()
    tiles_copy = pair(tiles.at[other], blocks.at[1], 2)
    tiles_copy.start()

    put_rows(cover_rows, None, demand)
    demand_here = cover_rows[...]

    row_ids, col_ids, row_marks, col_marks = [], [], [], []

    def take_ids(row_of, col_of, count):
        for j in range(slots):
            row, col = row_of(j), col_of(j)
            row_ids.append(row)
            col_ids.append(col)
            row_marks.append(jnp.where(j < count, row, -1))
            col_marks.append(jnp.where(j < count, col, -1))

    take_ids(
        lambda j: row_index[here, 0, 0, j],
        lambda j: col_index[here, 0, 0, j],
        tile_count[here, 0, 0],
    )
    ids_copy.wait()
    take_ids(lambda j: ids_in[j], lambda j: ids_in[slots + j], ids_in[2 * slots])

    lane_iota = lax.broadcasted_iota(jnp.int32, (row_blocks, tile), 0)
    col_iota = lax.broadcasted_iota(jnp.int32, (col_blocks, tile), 0)

    def spread(row, iota, mark):
        return jnp.where(iota == mark, jnp.broadcast_to(row, iota.shape), 0.0).astype(jnp.bfloat16)

    def backward(cover):
        cover_rows[...] = cover
        halves = []
        for half in range(2):
            acc = None
            for j in range(slots):
                n = half * slots + j
                row = cover_rows[pl.ds(row_ids[n], 1), :]
                part = dot(spread(row, col_iota, col_marks[n]), blocks[half, j])
                acc = part if acc is None else acc + part
            halves.append(acc)
        return jnp.concatenate(halves, axis=0)

    def forward(extrap):
        dispatch_rows[...] = extrap
        acc = None
        for half in range(2):
            for j in range(slots):
                n = half * slots + j
                row = dispatch_rows[pl.ds(half * col_blocks + col_ids[n], 1), :]
                part = dot_t(spread(row, lane_iota, row_marks[n]), blocks[half, j])
                acc = part if acc is None else acc + part
        return acc

    def group(source, target, k, at):
        to, device = member(k)
        return pltpu.make_async_remote_copy(
            src_ref=source.at[pl.ds(pl.multiple_of(8 * to, 8), 8)],
            dst_ref=target.at[pl.ds(pl.multiple_of(8 * me, 8), 8)],
            send_sem=group_send.at[at],
            recv_sem=group_recv.at[at],
            device_id=device,
            device_id_type=MESH,
        )

    def group_start(source, target, at):
        for k in range(1, members):
            group(source, target, k, at).start()
        mine = pl.ds(pl.multiple_of(8 * me, 8), 8)
        target[mine, :] = source[mine, :]

    def group_all(source, target, at):
        part = pl.ds(0, 8 * (members - 1))
        return pltpu.make_async_remote_copy(
            src_ref=source.at[part],
            dst_ref=target.at[part],
            send_sem=group_send.at[at],
            recv_sem=group_recv.at[at],
            device_id={"dep": other},
            device_id_type=MESH,
        )

    def in_order(x):
        own, far = x[:col_blocks], x[col_blocks:]
        first = here == 0
        return jnp.where(first, own, far), jnp.where(first, far, own)

    def kind(k):
        return pl.ds(k, members, stride=8)

    def gather_start(hedge_round, fleet, assign):
        buffer = gather_out.at[hedge_round]
        values = in_order(fleet) + in_order(assign)
        for k, value in enumerate(values):
            buffer[kind(k), :] = value
        branch = branch_of[here].astype(jnp.float32)
        buffer[kind(4), :] = jnp.full((members, tile), branch, jnp.float32)
        for k in range(5, 8):
            buffer[kind(k), :] = jnp.zeros((members, tile), jnp.float32)
        group_start(buffer, gather_in.at[hedge_round], hedge_round)

    def reply_start(hedge_round):
        group_all(gather_out.at[hedge_round], gather_in.at[hedge_round], hedge_round).wait_recv()
        buffer = gather_in.at[hedge_round]
        lanes = lax.broadcasted_iota(jnp.int32, (members, tile), 1).astype(jnp.float32)
        hot = (buffer[kind(4), :] == lanes).astype(jnp.bfloat16)
        same = dot_t(hot, hot).astype(jnp.bfloat16)
        parts = []
        for k in (2, 3):
            value = buffer[kind(k), :]
            high = value.astype(jnp.bfloat16)
            rest = value - high.astype(jnp.float32)
            middle = rest.astype(jnp.bfloat16)
            low = (rest - middle.astype(jnp.float32)).astype(jnp.bfloat16)
            parts += [high, middle, low]
        sums = dot(same, jnp.concatenate(parts, axis=1))
        pieces = [sums[:, i * tile : (i + 1) * tile] for i in range(6)]
        mean_0 = ((pieces[2] + pieces[1]) + pieces[0]) / per_branch
        mean_1 = ((pieces[5] + pieces[4]) + pieces[3]) / per_branch
        fleet_0, fleet_1 = (
            jnp.broadcast_to(
                jnp.sum(buffer[kind(k), :], axis=0, keepdims=True) / total_scen, (members, tile)
            )
            for k in (0, 1)
        )
        if hedge_round < ITERS - 1:
            values = [fleet_0, fleet_1, mean_0, mean_1]
        else:
            even = lax.rem(lax.broadcasted_iota(jnp.int32, (members, tile), 0), 2) == 0
            down = jnp.concatenate([mean_1[-1:], mean_1[:-1]], axis=0)
            up = jnp.concatenate([mean_0[1:], mean_0[:1]], axis=0)
            values = [
                jnp.where(even, fleet_0, fleet_1),
                jnp.where(even, mean_0, down),
                jnp.where(even, up, mean_1),
            ]
        out = reply_out.at[hedge_round]
        for k in range(8):
            out[kind(k), :] = values[k] if k < len(values) else jnp.zeros((members, tile), jnp.float32)
        group_start(out, reply_in.at[hedge_round], ITERS + hedge_round)

    def reply_wait(hedge_round):
        group_all(reply_out.at[hedge_round], reply_in.at[hedge_round], ITERS + hedge_round).wait_recv()

    zeros = jnp.zeros((2 * col_blocks, tile), jnp.float32)
    fleet = assign = dispatch = fleet_dual = assign_dual = fleet_price = assign_price = zeros
    fleet_mean = assign_mean = zeros
    cover = jnp.zeros((row_blocks, tile), jnp.float32)
    ratio = jnp.ones((1, 1), jnp.float32)
    costs_copy.wait()
    branch_c = jnp.concatenate([costs[0, 0], costs[1, 0]], axis=0)
    dispatch_c = jnp.concatenate([costs[0, 1], costs[1, 1]], axis=0)
    root_c = jnp.concatenate([costs[0, 2], costs[1, 2]], axis=0)
    own_tiles.wait()
    tiles_copy.wait()

    for hedge_round in range(ITERS):
        penalty_now = 0.0 if hedge_round == 0 else penalty
        for inner_step in range(STEPS):
            ends = inner_step == STEPS - 1
            closing = hedge_round == ITERS - 1 and ends
            waits = hedge_round > 0 and inner_step == 0
            primal_step = step_scale / ratio
            dual_step = step_scale * ratio

            def plans():
                pull_f = root_c + fleet_price - fleet_dual
                pull_a = branch_c + assign_price + fleet_dual - assign_dual
                if penalty_now:
                    pull_f = pull_f + penalty_now * (fleet - fleet_mean)
                    pull_a = pull_a + penalty_now * (assign - assign_mean)
                return (
                    jnp.maximum(0.0, fleet - primal_step * pull_f),
                    jnp.maximum(0.0, assign - primal_step * pull_a),
                )

            if not waits:
                fleet_new, assign_new = plans()
            if ends:
                gather_start(hedge_round, fleet_new, assign_new)
            if closing:
                for k, x in enumerate((fleet_new, assign_new, fleet_price, assign_price)):
                    early_out[k] = x[col_blocks:]
                early_copy = pair(early_out, early_in, 3)
                early_copy.start()
            first = hedge_round == 0 and inner_step == 0
            pulled = zeros if first else backward(cover)
            dispatch_new = jnp.maximum(0.0, dispatch - primal_step * (dispatch_c + assign_dual - pulled))
            dispatch_ext = 2.0 * dispatch_new - dispatch
            load = forward(dispatch_ext)
            cover_new = jnp.maximum(0.0, cover + dual_step * (demand_here - load))
            if closing:
                late_out[0] = dispatch_new[col_blocks:]
                late_out[1] = cover_new
                late_copy = pair(late_out, late_in, 4)
                late_copy.start()
            if waits:
                reply_wait(hedge_round - 1)
                back = reply_in.at[hedge_round - 1]
                fleet_mean = jnp.concatenate(in_order(jnp.concatenate([back[kind(0), :], back[kind(1), :]], axis=0)), axis=0)
                assign_mean = jnp.concatenate(in_order(jnp.concatenate([back[kind(2), :], back[kind(3), :]], axis=0)), axis=0)
                fleet_price = fleet_price + penalty * (fleet - fleet_mean)
                assign_price = assign_price + penalty * (assign - assign_mean)
                fleet_new, assign_new = plans()
            if not closing:
                fleet_ext = 2.0 * fleet_new - fleet
                assign_ext = 2.0 * assign_new - assign
                assign_dual_new = jnp.maximum(0.0, assign_dual + dual_step * (dispatch_ext - assign_ext))
                fleet_dual_new = jnp.maximum(0.0, fleet_dual + dual_step * (assign_ext - fleet_ext))
                primal_moves = total(
                    (fleet_new - fleet) ** 2 + (assign_new - assign) ** 2 + (dispatch_new - dispatch) ** 2
                )
                pair_moves = total((assign_dual_new - assign_dual) ** 2 + (fleet_dual_new - fleet_dual) ** 2)
                cover_moves = total((cover_new - cover) ** 2)
                primal_rate = primal_moves / (3.0 * col_total)
                dual_rate = (cover_moves + pair_moves) / (lane_total + 2.0 * col_total)
                target = jnp.sqrt((primal_rate + epsilon) / (dual_rate + epsilon))
                ratio = jnp.sqrt(ratio * target)
                fleet_dual, assign_dual = fleet_dual_new, assign_dual_new
            fleet, assign, dispatch, cover = fleet_new, assign_new, dispatch_new, cover_new
            if ends:
                reply_start(hedge_round)

    def put_out(ref, own, far):
        row_0, row_1 = jnp.where(here == 0, own, far), jnp.where(here == 0, far, own)
        for c in range(own.shape[0]):
            ref[0:1, c * tile : (c + 1) * tile] = row_0[c : c + 1]
            ref[1:2, c * tile : (c + 1) * tile] = row_1[c : c + 1]

    early_copy.wait()
    put_out(fleet_out, fleet[:col_blocks], early_in[0])
    put_out(assign_out, assign[:col_blocks], early_in[1])
    late_copy.wait()
    put_out(dispatch_out, dispatch[:col_blocks], late_in[0])
    put_out(cover_out, cover, late_in[1])
    reply_wait(ITERS - 1)
    back = reply_in.at[ITERS - 1]
    last_fleet = back[kind(0), :]
    even_mean, odd_mean = back[kind(1), :], back[kind(2), :]
    own_mean = jnp.where(here == 0, even_mean, odd_mean)
    far_mean = jnp.where(here == 0, odd_mean, even_mean)
    put_out(
        fleet_price_out,
        fleet_price[:col_blocks] + penalty * (fleet[:col_blocks] - last_fleet),
        early_in[2] + penalty * (early_in[0] - last_fleet),
    )
    put_out(
        assign_price_out,
        assign_price[:col_blocks] + penalty * (assign[:col_blocks] - own_mean),
        early_in[3] + penalty * (early_in[1] - far_mean),
    )
    for r in range(ITERS):
        group_all(gather_out.at[r], gather_in.at[r], r).wait_send()
        group_all(reply_out.at[r], reply_in.at[r], ITERS + r).wait_send()


def fused_local(
    n_scen,
    tiles,
    row_index,
    col_index,
    tile_count,
    demand,
    root_cost,
    branch_cost,
    dispatch_cost,
    branch_of,
):
    slots, tile = tiles.shape[3], tiles.shape[5]
    lane_rows, width = demand.shape[1], branch_cost.shape[1]
    rows, cols, members = lane_rows // tile, width // tile, 2 * n_scen
    f32 = jnp.float32
    vmem = pl.BlockSpec(memory_space=pltpu.VMEM)
    smem = pl.BlockSpec(memory_space=pltpu.SMEM)
    col_shape = jax.ShapeDtypeStruct((2, width), f32)
    lane_shape = jax.ShapeDtypeStruct((2, lane_rows), f32)
    return pl.pallas_call(
        functools.partial(fused, n_scen),
        out_shape=(col_shape, col_shape, col_shape, lane_shape, col_shape, col_shape),
        in_specs=[pl.BlockSpec(memory_space=pl.ANY), smem, smem, smem, vmem, vmem, vmem, vmem, smem],
        out_specs=(vmem,) * 6,
        scratch_shapes=[
            pltpu.VMEM((2, slots, tile, tile), jnp.bfloat16),
            pltpu.VMEM((3, cols, tile), f32),
            pltpu.VMEM((2, 3, cols, tile), f32),
            pltpu.SMEM((4 * slots,), jnp.int32),
            pltpu.SMEM((4 * slots,), jnp.int32),
            pltpu.VMEM((rows, tile), f32),
            pltpu.VMEM((2 * cols, tile), f32),
            pltpu.VMEM((ITERS, 8 * members, tile), f32),
            pltpu.VMEM((ITERS, 8 * members, tile), f32),
            pltpu.VMEM((ITERS, 8 * members, tile), f32),
            pltpu.VMEM((ITERS, 8 * members, tile), f32),
            pltpu.VMEM((4, cols, tile), f32),
            pltpu.VMEM((4, cols, tile), f32),
            pltpu.VMEM((2, cols, tile), f32),
            pltpu.VMEM((2, cols, tile), f32),
            pltpu.SemaphoreType.DMA,
            pltpu.SemaphoreType.DMA((5,)),
            pltpu.SemaphoreType.DMA((5,)),
            pltpu.SemaphoreType.DMA((2 * ITERS,)),
            pltpu.SemaphoreType.DMA((2 * ITERS,)),
        ],
        compiler_params=pltpu.CompilerParams(
            collective_id=0, has_side_effects=True, vmem_limit_bytes=16 * 1024 * 1024
        ),
    )(
        tiles.reshape(2, slots, tile, tile),
        row_index,
        col_index,
        tile_count,
        demand,
        root_cost.reshape(cols, tile),
        branch_cost,
        dispatch_cost,
        branch_of,
    )


def solution_body(mesh):
    n_scen = mesh.shape["scen"]
    fits = mesh.shape["lane"] == 1 and mesh.shape["dep"] == 2 and (2 * n_scen) % BRANCHES == 0

    def body(*args):
        tiles, demand, root_cost = args[0], args[4], args[5]
        tile = tiles.shape[5]
        cols, rows = root_cost.shape[0] // tile, demand.shape[1] // tile
        if fits and tiles.shape[0] == 2 and tile == 128 and cols == rows == 2 * n_scen and cols % 8 == 0:
            return fused_local(n_scen, *args)
        return local(*args)

    return body


def solution(mesh):
    in_specs = (
        P(("groups", "scen"), "lane", "dep", None, None, None),
        P(("groups", "scen"), "lane", "dep", None),
        P(("groups", "scen"), "lane", "dep", None),
        P(("groups", "scen"), "lane", "dep"),
        P(("groups", "scen"), "lane"),
        P(("groups", "dep")),
        P(("groups", "scen"), "dep"),
        P(("groups", "scen"), "dep"),
        P(("groups", "scen")),
    )
    out_specs = (
        P(("groups", "scen"), "dep"),
        P(("groups", "scen"), "dep"),
        P(("groups", "scen"), "dep"),
        P(("groups", "scen"), "lane"),
        P(("groups", "scen"), "dep"),
        P(("groups", "scen"), "dep"),
    )
    body = solution_body(mesh)
    return jax.shard_map(body, mesh=mesh, in_specs=in_specs, out_specs=out_specs, check_vma=False)
```

profile of v0, /device:TPU:0, one launch (start us, length us, event | category | flops | bytes accessed | tf_op | source)
XLA Modules:
  0.0 40.0 jit_solution(17351969406842809646)
XLA Ops:
  0.6 0.0 copy-start.8
  0.6 0.0 copy-start.6
  0.7 0.6 %copy-done.8 = s32[2,1,1]{0,2,1:T(1,128)S(1)} copy-done((s32[2,1,1]{0,2,1:T(1,128)S(1)}, s32[2,1,1]{0,2,1:T(1,128)}, u32[]{:S(2)}) %copy-start.8) | copy-done | bytes 32
  1.3 0.0 copy-start.5
  1.3 0.0 copy-start.7
  1.3 0.1 copy.15.tile_count
  1.4 0.0 copy-done.6
  1.4 0.6 %copy-done.5 = s32[2,1,1,8]{3,2,1,0:T(1,128)S(1)} copy-done((s32[2,1,1,8]{3,2,1,0:T(1,128)S(1)}, s32[2,1,1,8]{3,2,1,0:T(1,128)}, u32[]{:S(2)}) %copy-start.5) | copy-done | bytes 88
  2.0 0.0 copy-done.7
  2.0 0.0 copy-start
  2.0 1.0 %copy-done = bf16[2,1,1,8,128,128]{5,4,3,2,1,0:T(8,128)(2,1)S(1)} copy-done((bf16[2,1,1,8,128,128]{5,4,3,2,1,0:T(8,128)(2,1)S(1)}, bf16[2,1,1,8,128,128]{5,4,3,2,1,0:T(8,128)(2,1)}, u32[]{:S(2)}) %copy-start) | copy-done | bytes 524312
  3.0 0.0 copy-start.1
  3.0 0.7 %copy-done.1 = f32[2,2048]{1,0:T(2,128)S(1)} copy-done((f32[2,2048]{1,0:T(2,128)S(1)}, f32[2,2048]{1,0:T(2,128)}, u32[]{:S(2)}) %copy-start.1) | copy-done | bytes 16408
  3.7 0.0 copy-start.2
  3.7 0.7 %copy-done.2 = f32[2,2048]{1,0:T(2,128)S(1)} copy-done((f32[2,2048]{1,0:T(2,128)S(1)}, f32[2,2048]{1,0:T(2,128)}, u32[]{:S(2)}) %copy-start.2) | copy-done | bytes 16408
  4.5 0.0 copy-start.3
  4.5 0.7 %copy-done.3 = f32[2,2048]{1,0:T(2,128)S(1)} copy-done((f32[2,2048]{1,0:T(2,128)S(1)}, f32[2,2048]{1,0:T(2,128)}, u32[]{:S(2)}) %copy-start.3) | copy-done | bytes 16408
  5.2 0.0 copy-start.4
  5.2 0.7 %copy-done.4 = f32[2048]{0:T(1024)S(1)} copy-done((f32[2048]{0:T(1024)S(1)}, f32[2048]{0:T(1024)}, u32[]{:S(2)}) %copy-start.4) | copy-done | bytes 8216
  5.9 30.5 %shard_map.136 = (f32[2,2048]{1,0:T(2,128)S(1)}, f32[2,2048]{1,0:T(2,128)S(1)}, f32[2,2048]{1,0:T(2,128)S(1)}, f32[2,2048]{1,0:T(2,128)S(1)}, f32[2,2048]{1,0:T(2,128)S(1)}, /*index=5*/f32[2,2048]{1,0:T(2,128)S(1)}) custom-call(bf16[2,8,128,128]{3,2,1,0:T(8,128)(2,1)S(1)} %bitcast.2, s32[2,1,1,8]{3,2,1,0:T(1,128)S(1)} %copy-done.5, ...), custom_call_target="tpu_custom_call" | custom-call | tf_op jit(solution)/shard_map/pallas_call | solution.py:561
  36.4 0.6 %copy.22 = f32[2,2048]{1,0:T(2,128)} copy(f32[2,2048]{1,0:T(2,128)S(1)} %get-tuple-element.12) | data formatting | bytes 32768
  37.0 0.6 %copy.23 = f32[2,2048]{1,0:T(2,128)} copy(f32[2,2048]{1,0:T(2,128)S(1)} %get-tuple-element.13) | data formatting | bytes 32768
  37.6 0.6 %copy.24 = f32[2,2048]{1,0:T(2,128)} copy(f32[2,2048]{1,0:T(2,128)S(1)} %get-tuple-element.14) | data formatting | bytes 32768
  38.2 0.6 %copy.25 = f32[2,2048]{1,0:T(2,128)} copy(f32[2,2048]{1,0:T(2,128)S(1)} %get-tuple-element.15) | data formatting | bytes 32768
  38.8 0.6 %copy.26 = f32[2,2048]{1,0:T(2,128)} copy(f32[2,2048]{1,0:T(2,128)S(1)} %get-tuple-element.16) | data formatting | bytes 32768
  39.4 0.6 %copy.27 = f32[2,2048]{1,0:T(2,128)} copy(f32[2,2048]{1,0:T(2,128)S(1)} %get-tuple-element.17) | data formatting | bytes 32768
Async XLA Ops:
  0.6 0.7 %copy-start.8 = (s32[2,1,1]{0,2,1:T(1,128)S(1)}, s32[2,1,1]{0,2,1:T(1,128)}, u32[]{:S(2)}) copy-start(s32[2,1,1]{0,2,1:T(1,128)} %param.12) | copy-start | bytes 28
  0.6 0.7 %copy-start.6 = (s32[2,1,1,8]{3,2,1,0:T(1,128)S(1)}, s32[2,1,1,8]{3,2,1,0:T(1,128)}, u32[]{:S(2)}) copy-start(s32[2,1,1,8]{3,2,1,0:T(1,128)} %col_index.1) | copy-start | bytes 196
  1.3 0.7 %copy-start.5 = (s32[2,1,1,8]{3,2,1,0:T(1,128)S(1)}, s32[2,1,1,8]{3,2,1,0:T(1,128)}, u32[]{:S(2)}) copy-start(s32[2,1,1,8]{3,2,1,0:T(1,128)} %row_index.1) | copy-start | bytes 196
  1.3 0.7 %copy-start.7 = (s32[2]{0:T(128)S(1)}, s32[2]{0:T(128)}, u32[]{:S(2)}) copy-start(s32[2]{0:T(128)} %branch_of.1) | copy-start | bytes 28
  2.0 1.0 %copy-start = (bf16[2,1,1,8,128,128]{5,4,3,2,1,0:T(8,128)(2,1)S(1)}, bf16[2,1,1,8,128,128]{5,4,3,2,1,0:T(8,128)(2,1)}, u32[]{:S(2)}) copy-start(bf16[2,1,1,8,128,128]{5,4,3,2,1,0:T(8,128)(2,1)} %param.9) | copy-start | bytes 1572868
  3.0 0.7 %copy-start.1 = (f32[2,2048]{1,0:T(2,128)S(1)}, f32[2,2048]{1,0:T(2,128)}, u32[]{:S(2)}) copy-start(f32[2,2048]{1,0:T(2,128)} %demand.1) | copy-start | bytes 49156
  3.7 0.7 %copy-start.2 = (f32[2,2048]{1,0:T(2,128)S(1)}, f32[2,2048]{1,0:T(2,128)}, u32[]{:S(2)}) copy-start(f32[2,2048]{1,0:T(2,128)} %branch_cost.1) | copy-start | bytes 49156
  4.5 0.7 %copy-start.3 = (f32[2,2048]{1,0:T(2,128)S(1)}, f32[2,2048]{1,0:T(2,128)}, u32[]{:S(2)}) copy-start(f32[2,2048]{1,0:T(2,128)} %dispatch_cost.1) | copy-start | bytes 49156
  5.2 0.7 %copy-start.4 = (f32[2048]{0:T(1024)S(1)}, f32[2048]{0:T(1024)}, u32[]{:S(2)}) copy-start(f32[2048]{0:T(1024)} %param.14) | copy-start | bytes 24580
where the time goes:
time: 40.6 us; the launch traced here: 40 us
  Pallas kernels  30.5 us (75%)
  local copies, waits for them, and re-layouts  8.84 us (22%)
  between operations  0.67 us (2%)
    pallas_call x1, Pallas kernels, fused_local(): pl.pallas_call(functools.partial(fused, n_scen), out_shape=(col_shape, co...  30.5 us
    unnamed x25, local copies, waits for them, and re-layouts  8.84 us

commit v1 on v0

--- a/solution.py
+++ b/solution.py
@@ -187,21 +187,25 @@
 def fused(
     n_scen,
     tiles,
+    row_index_in,
+    col_index_in,
+    tile_count_in,
+    demand_in,
+    root_cost_in,
+    branch_cost_in,
+    dispatch_cost_in,
+    branch_of_in,
+    packed,
     row_index,
     col_index,
     tile_count,
+    branch_of,
     demand,
     root_cost,
     branch_cost,
     dispatch_cost,
-    branch_of,
-    fleet_out,
-    assign_out,
-    dispatch_out,
-    cover_out,
-    fleet_price_out,
-    assign_price_out,
     blocks,
+    flipped,
     costs_out,
     costs,
     ids_out,
@@ -217,6 +221,7 @@
     late_out,
     late_in,
     local_sem,
+    load_sem,
     pair_send,
     pair_recv,
     group_send,
@@ -242,6 +247,21 @@
         to = lax.rem(me + k, members)
         return to, {"scen": to // 2, "dep": lax.rem(to, 2)}
 
+    def load(source, target, at):
+        copy = pltpu.make_async_copy(source, target, load_sem.at[at])
+        copy.start()
+        return copy
+
+    loads = [
+        load(row_index_in, row_index, 0),
+        load(col_index_in, col_index, 1),
+        load(tile_count_in, tile_count, 2),
+        load(branch_cost_in, branch_cost, 3),
+        load(dispatch_cost_in, dispatch_cost, 4),
+        load(root_cost_in, root_cost, 5),
+        load(demand_in, demand, 6),
+        load(branch_of_in, branch_of, 7),
+    ]
     barrier = pltpu.get_barrier_semaphore()
     for k in range(1, members):
         _, device = member(k)
@@ -258,6 +278,8 @@
             if far is not None:
                 far[c : c + 1, :] = jnp.where(here == 0, row_1, row_0)
 
+    for copy in loads:
+        copy.wait()
     put_rows(costs.at[0, 0], costs_out.at[0], branch_cost)
     put_rows(costs.at[0, 1], costs_out.at[1], dispatch_cost)
     costs_out[2] = root_cost[...]
@@ -265,7 +287,7 @@
     for j in range(slots):
         ids_out[j] = row_index[other, 0, 0, j]
         ids_out[slots + j] = col_index[other, 0, 0, j]
-    ids_out[2 * slots] = tile_count[other, 0, 0]
+    ids_out[2 * slots] = tile_count[other]
 
     def pair(source, target, at):
         return pltpu.make_async_remote_copy(
@@ -301,7 +323,7 @@
     take_ids(
         lambda j: row_index[here, 0, 0, j],
         lambda j: col_index[here, 0, 0, j],
-        tile_count[here, 0, 0],
+        tile_count[here],
     )
     ids_copy.wait()
     take_ids(lambda j: ids_in[j], lambda j: ids_in[slots + j], ids_in[2 * slots])
@@ -316,25 +338,24 @@
         cover_rows[...] = cover
         halves = []
         for half in range(2):
-            acc = None
-            for j in range(slots):
-                n = half * slots + j
+            left = []
+            for n in range(half * slots, (half + 1) * slots):
                 row = cover_rows[pl.ds(row_ids[n], 1), :]
-                part = dot(spread(row, col_iota, col_marks[n]), blocks[half, j])
-                acc = part if acc is None else acc + part
-            halves.append(acc)
+                left.append(spread(row, col_iota, col_marks[n]))
+            halves.append(dot(jnp.concatenate(left, axis=1), blocks[half].reshape(slots * tile, tile)))
         return jnp.concatenate(halves, axis=0)
 
     def forward(extrap):
         dispatch_rows[...] = extrap
-        acc = None
-        for half in range(2):
-            for j in range(slots):
-                n = half * slots + j
-                row = dispatch_rows[pl.ds(half * col_blocks + col_ids[n], 1), :]
-                part = dot_t(spread(row, lane_iota, row_marks[n]), blocks[half, j])
-                acc = part if acc is None else acc + part
-        return acc
+        left = []
+        for n in range(2 * slots):
+            row = dispatch_rows[pl.ds(n // slots * col_blocks + col_ids[n], 1), :]
+            left.append(spread(row, lane_iota, row_marks[n]))
+        return dot(jnp.concatenate(left, axis=1), flipped[...].reshape(2 * slots * tile, tile))
+
+    def flip(half):
+        for j in range(slots):
+            flipped[half, j] = blocks[half, j].T
 
     def group(source, target, k, at):
         to, device = member(k)
@@ -436,7 +457,9 @@
     dispatch_c = jnp.concatenate([costs[0, 1], costs[1, 1]], axis=0)
     root_c = jnp.concatenate([costs[0, 2], costs[1, 2]], axis=0)
     own_tiles.wait()
+    flip(0)
     tiles_copy.wait()
+    flip(1)
 
     for hedge_round in range(ITERS):
         penalty_now = 0.0 if hedge_round == 0 else penalty
@@ -505,18 +528,18 @@
             if ends:
                 reply_start(hedge_round)
 
-    def put_out(ref, own, far):
+    def put_out(at, own, far):
         row_0, row_1 = jnp.where(here == 0, own, far), jnp.where(here == 0, far, own)
         for c in range(own.shape[0]):
-            ref[0:1, c * tile : (c + 1) * tile] = row_0[c : c + 1]
-            ref[1:2, c * tile : (c + 1) * tile] = row_1[c : c + 1]
+            packed[at, 0:1, c * tile : (c + 1) * tile] = row_0[c : c + 1]
+            packed[at, 1:2, c * tile : (c + 1) * tile] = row_1[c : c + 1]
 
     early_copy.wait()
-    put_out(fleet_out, fleet[:col_blocks], early_in[0])
-    put_out(assign_out, assign[:col_blocks], early_in[1])
+    put_out(0, fleet[:col_blocks], early_in[0])
+    put_out(1, assign[:col_blocks], early_in[1])
     late_copy.wait()
-    put_out(dispatch_out, dispatch[:col_blocks], late_in[0])
-    put_out(cover_out, cover, late_in[1])
+    put_out(2, dispatch[:col_blocks], late_in[0])
+    put_out(3, cover, late_in[1])
     reply_wait(ITERS - 1)
     back = reply_in.at[ITERS - 1]
     last_fleet = back[kind(0), :]
@@ -524,18 +547,23 @@
     own_mean = jnp.where(here == 0, even_mean, odd_mean)
     far_mean = jnp.where(here == 0, odd_mean, even_mean)
     put_out(
-        fleet_price_out,
+        4,
         fleet_price[:col_blocks] + penalty * (fleet[:col_blocks] - last_fleet),
         early_in[2] + penalty * (early_in[0] - last_fleet),
     )
     put_out(
-        assign_price_out,
+        5,
         assign_price[:col_blocks] + penalty * (assign[:col_blocks] - own_mean),
         early_in[3] + penalty * (early_in[1] - far_mean),
     )
     for r in range(ITERS):
         group_all(gather_out.at[r], gather_in.at[r], r).wait_send()
         group_all(reply_out.at[r], reply_in.at[r], ITERS + r).wait_send()
+
+
+def unpack(packed, *outs):
+    for k, out in enumerate(outs):
+        out[...] = packed[k]
 
 
 def fused_local(
@@ -553,17 +581,24 @@
     slots, tile = tiles.shape[3], tiles.shape[5]
     lane_rows, width = demand.shape[1], branch_cost.shape[1]
     rows, cols, members = lane_rows // tile, width // tile, 2 * n_scen
-    f32 = jnp.float32
-    vmem = pl.BlockSpec(memory_space=pltpu.VMEM)
-    smem = pl.BlockSpec(memory_space=pltpu.SMEM)
+    f32, i32 = jnp.float32, jnp.int32
+    anywhere = pl.BlockSpec(memory_space=pl.ANY)
     col_shape = jax.ShapeDtypeStruct((2, width), f32)
-    lane_shape = jax.ShapeDtypeStruct((2, lane_rows), f32)
-    return pl.pallas_call(
+    packed = pl.pallas_call(
         functools.partial(fused, n_scen),
-        out_shape=(col_shape, col_shape, col_shape, lane_shape, col_shape, col_shape),
-        in_specs=[pl.BlockSpec(memory_space=pl.ANY), smem, smem, smem, vmem, vmem, vmem, vmem, smem],
-        out_specs=(vmem,) * 6,
+        out_shape=jax.ShapeDtypeStruct((6, 2, width), f32),
+        in_specs=[pl.BlockSpec(memory_space=pltpu.HBM)] * 9,
+        out_specs=pl.BlockSpec(memory_space=pltpu.VMEM),
         scratch_shapes=[
+            pltpu.SMEM(row_index.shape, i32),
+            pltpu.SMEM(col_index.shape, i32),
+            pltpu.SMEM((2,), i32),
+            pltpu.SMEM(branch_of.shape, i32),
+            pltpu.VMEM(demand.shape, f32),
+            pltpu.VMEM((cols, tile), f32),
+            pltpu.VMEM(branch_cost.shape, f32),
+            pltpu.VMEM(dispatch_cost.shape, f32),
+            pltpu.VMEM((2, slots, tile, tile), jnp.bfloat16),
             pltpu.VMEM((2, slots, tile, tile), jnp.bfloat16),
             pltpu.VMEM((3, cols, tile), f32),
             pltpu.VMEM((2, 3, cols, tile), f32),
@@ -580,25 +615,32 @@
             pltpu.VMEM((2, cols, tile), f32),
             pltpu.VMEM((2, cols, tile), f32),
             pltpu.SemaphoreType.DMA,
+            pltpu.SemaphoreType.DMA((8,)),
             pltpu.SemaphoreType.DMA((5,)),
             pltpu.SemaphoreType.DMA((5,)),
             pltpu.SemaphoreType.DMA((2 * ITERS,)),
             pltpu.SemaphoreType.DMA((2 * ITERS,)),
         ],
         compiler_params=pltpu.CompilerParams(
-            collective_id=0, has_side_effects=True, vmem_limit_bytes=16 * 1024 * 1024
+            collective_id=0, has_side_effects=True, vmem_limit_bytes=60 * 1024 * 1024
         ),
     )(
         tiles.reshape(2, slots, tile, tile),
         row_index,
         col_index,
-        tile_count,
+        tile_count.reshape(2),
         demand,
         root_cost.reshape(cols, tile),
         branch_cost,
         dispatch_cost,
         branch_of,
     )
+    return pl.pallas_call(
+        unpack,
+        out_shape=(col_shape,) * 6,
+        in_specs=[pl.BlockSpec(memory_space=pltpu.VMEM)],
+        out_specs=(pl.BlockSpec(memory_space=pltpu.VMEM),) * 6,
+    )(packed)
 
 
 def solution_body(mesh):

time: 40.6 us -> 30.2 us (0.74)
  local copies, waits for them, and re-layouts: 8.84 us -> 0 us
  Pallas kernels: 30.5 us -> 29.4 us
    unnamed x25 -> x0, local copies, waits for them, and re-layouts: 8.84 us -> none
    pallas_call x1 -> x2, Pallas kernels: 30.5 us -> 29.4 us  [the longest x1 27.8 us: fused_local(): pl.pallas_call(functools.partial(fused, n_scen), out_shape=jax.ShapeDtype...]
where the time goes in v1:
time: 30.2 us; the launch traced here: 30 us
  Pallas kernels  29.4 us (97%)
  between operations  0.64 us (2%)
    pallas_call x1, Pallas kernels, fused_local(): pl.pallas_call(functools.partial(fused, n_scen), out_shape=jax.ShapeDtype...  27.8 us
    pallas_call x1, Pallas kernels, fused_local(): pl.pallas_call(unpack, out_shape=(col_shape,) * 6, in_specs=[pl.BlockSpec...  1.53 us

profile of v1, /device:TPU:0, one launch (start us, length us, event | category | flops | bytes accessed | tf_op | source)
XLA Modules:
  0.0 30.0 jit_solution(406437630498740694)
XLA Ops:
  0.6 27.8 %shard_map.136.packed = f32[6,2,2048]{2,1,0:T(2,128)} custom-call(bf16[2,8,128,128]{3,2,1,0:T(8,128)(2,1)} %bitcast.3, s32[2,1,1,8]{3,2,1,0:T(1,128)} %row_index_in.1, s32[2,1,1,8]{3,2,1,0:T(1,128)} %col_index_in.1, s32[2]{0:T(128)} %bitcast.5, f32[2,2048]{1,0:T(2,128)} %demand_in.1, f32[16,128]{1,0:T(8,128)} %bitcast.4, f32[2,2048]{1,0:T(2,128)} %branch_cost_in.1, ...), custom_call_target="tpu_custom_call" | custom-call | tf_op jit(solution)/shard_map/pallas_call | solution.py:587
  28.5 1.5 %shard_map.137 = (f32[2,2048]{1,0:T(2,128)}, f32[2,2048]{1,0:T(2,128)}, f32[2,2048]{1,0:T(2,128)}, f32[2,2048]{1,0:T(2,128)}, f32[2,2048]{1,0:T(2,128)}, /*index=5*/f32[2,2048]{1,0:T(2,128)}) custom-call(f32[6,2,2048]{2,1,0:T(2,128)} %shard_map.136.packed), custom_call_target="tpu_custom_call" | custom-call | tf_op jit(solution)/shard_map/pallas_call | solution.py:638

commit v2 on v1

--- a/solution.py
+++ b/solution.py
@@ -216,6 +216,9 @@
     gather_in,
     reply_out,
     reply_in,
+    branch_out,
+    branch_in,
+    same_branch,
     early_out,
     early_in,
     late_out,
@@ -226,6 +229,7 @@
     pair_recv,
     group_send,
     group_recv,
+    entered,
 ):
     here = lax.axis_index("dep")
     other = 1 - here
@@ -243,9 +247,13 @@
     total_scen = float(members)
     per_branch = float(members // BRANCHES)
 
-    def member(k):
-        to = lax.rem(me + k, members)
-        return to, {"scen": to // 2, "dep": lax.rem(to, 2)}
+    owners = members // 2
+    first_owner = members // 4
+    owner = me - first_owner
+    owns = jnp.logical_and(owner >= 0, owner < owners)
+
+    def device_of(to):
+        return {"scen": to // 2, "dep": lax.rem(to, 2)}
 
     def load(source, target, at):
         copy = pltpu.make_async_copy(source, target, load_sem.at[at])
@@ -263,9 +271,14 @@
         load(branch_of_in, branch_of, 7),
     ]
     barrier = pltpu.get_barrier_semaphore()
-    for k in range(1, members):
-        _, device = member(k)
+    leads = here == 0
+    for k in range(1, n_scen):
+        device = {"scen": lax.rem(chip + k, n_scen), "dep": 1}
         pl.semaphore_signal(barrier, inc=1, device_id=device, device_id_type=MESH)
+
+    @pl.when(here == 1)
+    def _():
+        pl.semaphore_signal(barrier, inc=1, device_id={"dep": other}, device_id_type=MESH)
 
     own_tiles = pltpu.make_async_copy(tiles.at[here], blocks.at[0], local_sem)
     own_tiles.start()
@@ -299,13 +312,23 @@
             device_id_type=MESH,
         )
 
-    pl.semaphore_wait(barrier, members - 1)
     ids_copy = pair(ids_out, ids_in, 0)
-    ids_copy.start()
     costs_copy = pair(costs_out, costs.at[1], 1)
-    costs_copy.start()
     tiles_copy = pair(tiles.at[other], blocks.at[1], 2)
-    tiles_copy.start()
+
+    @pl.when(leads)
+    def _():
+        pl.semaphore_wait(barrier, 1)
+        tiles_copy.start()
+        ids_copy.start()
+        costs_copy.start()
+
+    @pl.when(here == 1)
+    def _():
+        ids_copy.wait_recv()
+        tiles_copy.start()
+        ids_copy.start()
+        costs_copy.start()
 
     put_rows(cover_rows, None, demand)
     demand_here = cover_rows[...]
@@ -325,7 +348,11 @@
         lambda j: col_index[here, 0, 0, j],
         tile_count[here],
     )
-    ids_copy.wait()
+    @pl.when(leads)
+    def _():
+        ids_copy.wait_recv()
+
+    ids_copy.wait_send()
     take_ids(lambda j: ids_in[j], lambda j: ids_in[slots + j], ids_in[2 * slots])
 
     lane_iota = lax.broadcasted_iota(jnp.int32, (row_blocks, tile), 0)
@@ -357,95 +384,150 @@
         for j in range(slots):
             flipped[half, j] = blocks[half, j].T
 
-    def group(source, target, k, at):
-        to, device = member(k)
+    def place(index):
+        return pl.ds(pl.multiple_of(8 * index, 8), 8)
+
+    def group(source, target, at, to):
         return pltpu.make_async_remote_copy(
-            src_ref=source.at[pl.ds(pl.multiple_of(8 * to, 8), 8)],
-            dst_ref=target.at[pl.ds(pl.multiple_of(8 * me, 8), 8)],
+            src_ref=source,
+            dst_ref=target,
             send_sem=group_send.at[at],
             recv_sem=group_recv.at[at],
-            device_id=device,
+            device_id=device_of(to),
             device_id_type=MESH,
         )
 
-    def group_start(source, target, at):
-        for k in range(1, members):
-            group(source, target, k, at).start()
-        mine = pl.ds(pl.multiple_of(8 * me, 8), 8)
-        target[mine, :] = source[mine, :]
-
-    def group_all(source, target, at):
-        part = pl.ds(0, 8 * (members - 1))
-        return pltpu.make_async_remote_copy(
-            src_ref=source.at[part],
-            dst_ref=target.at[part],
-            send_sem=group_send.at[at],
-            recv_sem=group_recv.at[at],
-            device_id={"dep": other},
-            device_id_type=MESH,
-        )
+    def many(buffer, count, at):
+        part = buffer.at[pl.ds(0, 8 * count)]
+        return group(part, part, at, me + 1 - 2 * here)
+
+    def either(mine, others):
+        @pl.when(owns)
+        def _():
+            mine()
+
+        @pl.when(jnp.logical_not(owns))
+        def _():
+            others()
 
     def in_order(x):
         own, far = x[:col_blocks], x[col_blocks:]
-        first = here == 0
-        return jnp.where(first, own, far), jnp.where(first, far, own)
-
-    def kind(k):
-        return pl.ds(k, members, stride=8)
+        return jnp.where(leads, own, far), jnp.where(leads, far, own)
+
+    def kind(k, count):
+        return pl.ds(k, count, stride=8)
+
+    def to_owners(send):
+        for k in range(owners):
+            to = first_owner + lax.rem(me - first_owner + members + k, owners)
+            if k:
+                send(to)
+            else:
+                pl.when(jnp.logical_not(owns))(functools.partial(send, to))
+
+    def branch_start():
+        branch_out[...] = jnp.full((1, tile), branch_of[here].astype(jnp.float32), jnp.float32)
+
+        def send(to):
+            group(branch_out, branch_in.at[me], 2 * ITERS, to).start()
+
+        to_owners(send)
+
+    def branch_wait(count, wait):
+        part = branch_in.at[pl.ds(0, count)]
+        wait(group(part, part, 2 * ITERS, me + 1 - 2 * here))
 
     def gather_start(hedge_round, fleet, assign):
         buffer = gather_out.at[hedge_round]
-        values = in_order(fleet) + in_order(assign)
-        for k, value in enumerate(values):
-            buffer[kind(k), :] = value
-        branch = branch_of[here].astype(jnp.float32)
-        buffer[kind(4), :] = jnp.full((members, tile), branch, jnp.float32)
-        for k in range(5, 8):
-            buffer[kind(k), :] = jnp.zeros((members, tile), jnp.float32)
-        group_start(buffer, gather_in.at[hedge_round], hedge_round)
+        target = gather_in.at[hedge_round]
+        for k, value in enumerate(in_order(fleet) + in_order(assign)):
+            buffer[kind(2 * k, owners), :] = value[:owners]
+            buffer[kind(2 * k + 1, owners), :] = value[owners:]
+
+        def send(to):
+            group(buffer.at[place(to - first_owner)], target.at[place(me)], hedge_round, to).start()
+
+        to_owners(send)
+
+        @pl.when(owns)
+        def _():
+            target[place(me), :] = buffer[place(owner), :]
 
     def reply_start(hedge_round):
-        group_all(gather_out.at[hedge_round], gather_in.at[hedge_round], hedge_round).wait_recv()
+        pl.when(owns)(functools.partial(reply, hedge_round))
+
+    def reply(hedge_round):
+        if hedge_round == 0:
+            branch_wait(members - 1, lambda copy: copy.wait_recv())
+            branch_in[me] = branch_out[...]
+            branches = jnp.concatenate([branch_in[k] for k in range(members)], axis=0)
+            lanes = lax.broadcasted_iota(jnp.int32, (members, tile), 1).astype(jnp.float32)
+            hot = (branches == lanes).astype(jnp.bfloat16)
+            same_branch[...] = dot_t(hot, hot)
+        many(gather_in.at[hedge_round], members - 1, hedge_round).wait_recv()
         buffer = gather_in.at[hedge_round]
-        lanes = lax.broadcasted_iota(jnp.int32, (members, tile), 1).astype(jnp.float32)
-        hot = (buffer[kind(4), :] == lanes).astype(jnp.bfloat16)
-        same = dot_t(hot, hot).astype(jnp.bfloat16)
         parts = []
-        for k in (2, 3):
-            value = buffer[kind(k), :]
+        for k in range(4, 8):
+            value = buffer[kind(k, members), :]
             high = value.astype(jnp.bfloat16)
             rest = value - high.astype(jnp.float32)
             middle = rest.astype(jnp.bfloat16)
             low = (rest - middle.astype(jnp.float32)).astype(jnp.bfloat16)
             parts += [high, middle, low]
-        sums = dot(same, jnp.concatenate(parts, axis=1))
-        pieces = [sums[:, i * tile : (i + 1) * tile] for i in range(6)]
-        mean_0 = ((pieces[2] + pieces[1]) + pieces[0]) / per_branch
-        mean_1 = ((pieces[5] + pieces[4]) + pieces[3]) / per_branch
-        fleet_0, fleet_1 = (
+        sums = dot(same_branch[...].astype(jnp.bfloat16), jnp.concatenate(parts, axis=1))
+        pieces = [sums[:, i * tile : (i + 1) * tile] for i in range(12)]
+        means = [
+            ((pieces[3 * k + 2] + pieces[3 * k + 1]) + pieces[3 * k]) / per_branch for k in range(4)
+        ]
+        fleets = [
             jnp.broadcast_to(
-                jnp.sum(buffer[kind(k), :], axis=0, keepdims=True) / total_scen, (members, tile)
-            )
-            for k in (0, 1)
-        )
+                jnp.sum(buffer[kind(k, members), :], axis=0, keepdims=True) / total_scen,
+                (members, tile),
+            )
+            for k in range(4)
+        ]
         if hedge_round < ITERS - 1:
-            values = [fleet_0, fleet_1, mean_0, mean_1]
+            values = fleets + means
         else:
             even = lax.rem(lax.broadcasted_iota(jnp.int32, (members, tile), 0), 2) == 0
-            down = jnp.concatenate([mean_1[-1:], mean_1[:-1]], axis=0)
-            up = jnp.concatenate([mean_0[1:], mean_0[:1]], axis=0)
-            values = [
-                jnp.where(even, fleet_0, fleet_1),
-                jnp.where(even, mean_0, down),
-                jnp.where(even, up, mean_1),
-            ]
-        out = reply_out.at[hedge_round]
-        for k in range(8):
-            out[kind(k), :] = values[k] if k < len(values) else jnp.zeros((members, tile), jnp.float32)
-        group_start(out, reply_in.at[hedge_round], ITERS + hedge_round)
+            down = [jnp.concatenate([x[-1:], x[:-1]], axis=0) for x in means[2:]]
+            up = [jnp.concatenate([x[1:], x[:1]], axis=0) for x in means[:2]]
+            values = [jnp.where(even, fleets[k], fleets[2 + k]) for k in range(2)]
+            values += [jnp.where(even, means[k], down[k]) for k in range(2)]
+            values += [jnp.where(even, up[k], means[2 + k]) for k in range(2)]
+            values += [jnp.zeros((members, tile), jnp.float32)] * 2
+        out, target = reply_out.at[hedge_round], reply_in.at[hedge_round]
+        for k, value in enumerate(values):
+            out[kind(k, members), :] = value
+        for k in range(1, members):
+            to = lax.rem(me + k, members)
+            group(out.at[place(to)], target.at[place(owner)], ITERS + hedge_round, to).start()
+        target[place(owner), :] = out[place(me), :]
 
     def reply_wait(hedge_round):
-        group_all(reply_out.at[hedge_round], reply_in.at[hedge_round], ITERS + hedge_round).wait_recv()
+        buffer, at = reply_in.at[hedge_round], ITERS + hedge_round
+        either(
+            lambda: many(buffer, owners - 1, at).wait_recv(),
+            lambda: many(buffer, owners, at).wait_recv(),
+        )
+
+    def reply_half(hedge_round, k):
+        back = reply_in.at[hedge_round]
+        return jnp.concatenate([back[kind(k, owners), :], back[kind(k + 1, owners), :]], axis=0)
+
+    def reply_all(hedge_round, k):
+        halves = jnp.concatenate([reply_half(hedge_round, k), reply_half(hedge_round, k + 2)], axis=0)
+        return jnp.concatenate(in_order(halves), axis=0)
+
+    def group_enter():
+        @pl.when(here == 1)
+        def _():
+            pl.semaphore_wait(barrier, members - 2)
+            pl.semaphore_signal(entered, inc=1, device_id={"dep": other}, device_id_type=MESH)
+
+        @pl.when(leads)
+        def _():
+            pl.semaphore_wait(entered, 1)
 
     zeros = jnp.zeros((2 * col_blocks, tile), jnp.float32)
     fleet = assign = dispatch = fleet_dual = assign_dual = fleet_price = assign_price = zeros
@@ -461,6 +543,7 @@
     tiles_copy.wait()
     flip(1)
 
+    pulled = zeros
     for hedge_round in range(ITERS):
         penalty_now = 0.0 if hedge_round == 0 else penalty
         for inner_step in range(STEPS):
@@ -483,6 +566,9 @@
 
             if not waits:
                 fleet_new, assign_new = plans()
+            if hedge_round == 0 and inner_step == STEPS - 2:
+                group_enter()
+                branch_start()
             if ends:
                 gather_start(hedge_round, fleet_new, assign_new)
             if closing:
@@ -490,12 +576,12 @@
                     early_out[k] = x[col_blocks:]
                 early_copy = pair(early_out, early_in, 3)
                 early_copy.start()
-            first = hedge_round == 0 and inner_step == 0
-            pulled = zeros if first else backward(cover)
             dispatch_new = jnp.maximum(0.0, dispatch - primal_step * (dispatch_c + assign_dual - pulled))
             dispatch_ext = 2.0 * dispatch_new - dispatch
             load = forward(dispatch_ext)
             cover_new = jnp.maximum(0.0, cover + dual_step * (demand_here - load))
+            if not closing:
+                pulled = backward(cover_new)
             if closing:
                 late_out[0] = dispatch_new[col_blocks:]
                 late_out[1] = cover_new
@@ -503,9 +589,8 @@
                 late_copy.start()
             if waits:
                 reply_wait(hedge_round - 1)
-                back = reply_in.at[hedge_round - 1]
-                fleet_mean = jnp.concatenate(in_order(jnp.concatenate([back[kind(0), :], back[kind(1), :]], axis=0)), axis=0)
-                assign_mean = jnp.concatenate(in_order(jnp.concatenate([back[kind(2), :], back[kind(3), :]], axis=0)), axis=0)
+                fleet_mean = reply_all(hedge_round - 1, 0)
+                assign_mean = reply_all(hedge_round - 1, 4)
                 fleet_price = fleet_price + penalty * (fleet - fleet_mean)
                 assign_price = assign_price + penalty * (assign - assign_mean)
                 fleet_new, assign_new = plans()
@@ -541,9 +626,8 @@
     put_out(2, dispatch[:col_blocks], late_in[0])
     put_out(3, cover, late_in[1])
     reply_wait(ITERS - 1)
-    back = reply_in.at[ITERS - 1]
-    last_fleet = back[kind(0), :]
-    even_mean, odd_mean = back[kind(1), :], back[kind(2), :]
+    last_fleet = reply_half(ITERS - 1, 0)
+    even_mean, odd_mean = reply_half(ITERS - 1, 2), reply_half(ITERS - 1, 4)
     own_mean = jnp.where(here == 0, even_mean, odd_mean)
     far_mean = jnp.where(here == 0, odd_mean, even_mean)
     put_out(
@@ -556,9 +640,19 @@
         assign_price[:col_blocks] + penalty * (assign[:col_blocks] - own_mean),
         early_in[3] + penalty * (early_in[1] - far_mean),
     )
-    for r in range(ITERS):
-        group_all(gather_out.at[r], gather_in.at[r], r).wait_send()
-        group_all(reply_out.at[r], reply_in.at[r], ITERS + r).wait_send()
+
+    def sent_by_owner():
+        branch_wait(owners - 1, lambda copy: copy.wait_send())
+        for r in range(ITERS):
+            many(gather_in.at[r], owners - 1, r).wait_send()
+            many(gather_in.at[r], members - 1, ITERS + r).wait_send()
+
+    def sent_by_others():
+        branch_wait(owners, lambda copy: copy.wait_send())
+        for r in range(ITERS):
+            many(gather_in.at[r], owners, r).wait_send()
+
+    either(sent_by_owner, sent_by_others)
 
 
 def unpack(packed, *outs):
@@ -606,10 +700,13 @@
             pltpu.SMEM((4 * slots,), jnp.int32),
             pltpu.VMEM((rows, tile), f32),
             pltpu.VMEM((2 * cols, tile), f32),
+            pltpu.VMEM((ITERS, 4 * members, tile), f32),
             pltpu.VMEM((ITERS, 8 * members, tile), f32),
             pltpu.VMEM((ITERS, 8 * members, tile), f32),
-            pltpu.VMEM((ITERS, 8 * members, tile), f32),
-            pltpu.VMEM((ITERS, 8 * members, tile), f32),
+            pltpu.VMEM((ITERS, 4 * members, tile), f32),
+            pltpu.VMEM((1, tile), f32),
+            pltpu.VMEM((members, 1, tile), f32),
+            pltpu.VMEM((members, members), f32),
             pltpu.VMEM((4, cols, tile), f32),
             pltpu.VMEM((4, cols, tile), f32),
             pltpu.VMEM((2, cols, tile), f32),
@@ -618,8 +715,9 @@
             pltpu.SemaphoreType.DMA((8,)),
             pltpu.SemaphoreType.DMA((5,)),
             pltpu.SemaphoreType.DMA((5,)),
-            pltpu.SemaphoreType.DMA((2 * ITERS,)),
-            pltpu.SemaphoreType.DMA((2 * ITERS,)),
+            pltpu.SemaphoreType.DMA((2 * ITERS + 1,)),
+            pltpu.SemaphoreType.DMA((2 * ITERS + 1,)),
+            pltpu.SemaphoreType.REGULAR,
         ],
         compiler_params=pltpu.CompilerParams(
             collective_id=0, has_side_effects=True, vmem_limit_bytes=60 * 1024 * 1024

time: 30.2 us -> 27.1 us (0.90)
  Pallas kernels: 29.4 us -> 26.3 us
    pallas_call x1, Pallas kernels: 27.8 us -> 24.7 us  [fused_local(): pl.pallas_call(functools.partial(fused, n_scen), out_shape=jax.ShapeDtype...]
where the time goes in v2:
time: 27.1 us; the launch traced here: 26.9 us
  Pallas kernels  26.3 us (97%)
  between operations  0.64 us (2%)
    pallas_call x1, Pallas kernels, fused_local(): pl.pallas_call(functools.partial(fused, n_scen), out_shape=jax.ShapeDtype...  24.7 us
    pallas_call x1, Pallas kernels, fused_local(): pl.pallas_call(unpack, out_shape=(col_shape,) * 6, in_specs=[pl.BlockSpec...  1.53 us

profile of v2, /device:TPU:0, one launch (start us, length us, event | category | flops | bytes accessed | tf_op | source)
XLA Modules:
  0.0 26.9 jit_solution(17232113682324640439)
XLA Ops:
  0.6 24.7 %shard_map.136.packed = f32[6,2,2048]{2,1,0:T(2,128)} custom-call(bf16[2,8,128,128]{3,2,1,0:T(8,128)(2,1)} %bitcast.3, s32[2,1,1,8]{3,2,1,0:T(1,128)} %row_index_in.1, s32[2,1,1,8]{3,2,1,0:T(1,128)} %col_index_in.1, s32[2]{0:T(128)} %bitcast.5, f32[2,2048]{1,0:T(2,128)} %demand_in.1, f32[16,128]{1,0:T(8,128)} %bitcast.4, f32[2,2048]{1,0:T(2,128)} %branch_cost_in.1, ...), custom_call_target="tpu_custom_call" | custom-call | tf_op jit(solution)/shard_map/pallas_call | solution.py:681
  25.4 1.5 %shard_map.137 = (f32[2,2048]{1,0:T(2,128)}, f32[2,2048]{1,0:T(2,128)}, f32[2,2048]{1,0:T(2,128)}, f32[2,2048]{1,0:T(2,128)}, f32[2,2048]{1,0:T(2,128)}, /*index=5*/f32[2,2048]{1,0:T(2,128)}) custom-call(f32[6,2,2048]{2,1,0:T(2,128)} %shard_map.136.packed), custom_call_target="tpu_custom_call" | custom-call | tf_op jit(solution)/shard_map/pallas_call | solution.py:736

commit v3 on v2

--- a/solution.py
+++ b/solution.py
@@ -230,6 +230,7 @@
     group_send,
     group_recv,
     entered,
+    met,
 ):
     here = lax.axis_index("dep")
     other = 1 - here
@@ -280,9 +281,6 @@
     def _():
         pl.semaphore_signal(barrier, inc=1, device_id={"dep": other}, device_id_type=MESH)
 
-    own_tiles = pltpu.make_async_copy(tiles.at[here], blocks.at[0], local_sem)
-    own_tiles.start()
-
     def put_rows(own, far, source):
         for c in range(source.shape[1] // tile):
             row_0 = source[0:1, c * tile : (c + 1) * tile]
@@ -291,6 +289,32 @@
             if far is not None:
                 far[c : c + 1, :] = jnp.where(here == 0, row_1, row_0)
 
+    def pair(source, target, at):
+        return pltpu.make_async_remote_copy(
+            src_ref=source,
+            dst_ref=target,
+            send_sem=pair_send.at[at],
+            recv_sem=pair_recv.at[at],
+            device_id={"dep": other},
+            device_id_type=MESH,
+        )
+
+    ids_copy = pair(ids_out, ids_in, 0)
+    costs_copy = pair(costs_out, costs.at[1], 1)
+    tiles_copy = pair(tiles.at[other], blocks.at[1], 2)
+
+    @pl.when(leads)
+    def _():
+        pl.semaphore_wait(barrier, 1)
+        pl.semaphore_signal(met, inc=1, device_id={"dep": other}, device_id_type=MESH)
+
+    @pl.when(here == 1)
+    def _():
+        pl.semaphore_wait(met, 1)
+
+    tiles_copy.start()
+    own_tiles = pltpu.make_async_copy(tiles.at[here], blocks.at[0], local_sem)
+    own_tiles.start()
     for copy in loads:
         copy.wait()
     put_rows(costs.at[0, 0], costs_out.at[0], branch_cost)
@@ -302,33 +326,8 @@
         ids_out[slots + j] = col_index[other, 0, 0, j]
     ids_out[2 * slots] = tile_count[other]
 
-    def pair(source, target, at):
-        return pltpu.make_async_remote_copy(
-            src_ref=source,
-            dst_ref=target,
-            send_sem=pair_send.at[at],
-            recv_sem=pair_recv.at[at],
-            device_id={"dep": other},
-            device_id_type=MESH,
-        )
-
-    ids_copy = pair(ids_out, ids_in, 0)
-    costs_copy = pair(costs_out, costs.at[1], 1)
-    tiles_copy = pair(tiles.at[other], blocks.at[1], 2)
-
-    @pl.when(leads)
-    def _():
-        pl.semaphore_wait(barrier, 1)
-        tiles_copy.start()
-        ids_copy.start()
-        costs_copy.start()
-
-    @pl.when(here == 1)
-    def _():
-        ids_copy.wait_recv()
-        tiles_copy.start()
-        ids_copy.start()
-        costs_copy.start()
+    ids_copy.start()
+    costs_copy.start()
 
     put_rows(cover_rows, None, demand)
     demand_here = cover_rows[...]
@@ -348,11 +347,7 @@
         lambda j: col_index[here, 0, 0, j],
         tile_count[here],
     )
-    @pl.when(leads)
-    def _():
-        ids_copy.wait_recv()
-
-    ids_copy.wait_send()
+    ids_copy.wait()
     take_ids(lambda j: ids_in[j], lambda j: ids_in[slots + j], ids_in[2 * slots])
 
     lane_iota = lax.broadcasted_iota(jnp.int32, (row_blocks, tile), 0)
@@ -418,8 +413,10 @@
         return pl.ds(k, count, stride=8)
 
     def to_owners(send):
-        for k in range(owners):
-            to = first_owner + lax.rem(me - first_owner + members + k, owners)
+        half = owners // 2
+        home = me // half // 2 * half + lax.rem(me, half)
+        for k in reversed(range(owners)):
+            to = first_owner + jnp.bitwise_xor(home, k)
             if k:
                 send(to)
             else:
@@ -499,8 +496,10 @@
         out, target = reply_out.at[hedge_round], reply_in.at[hedge_round]
         for k, value in enumerate(values):
             out[kind(k, members), :] = value
-        for k in range(1, members):
-            to = lax.rem(me + k, members)
+        quarter = members // 4
+        near_last = [2, 3, 1, 0]
+        for k in sorted(range(1, members), key=lambda k: (near_last.index(k // quarter), -k)):
+            to = jnp.bitwise_xor(me, k)
             group(out.at[place(to)], target.at[place(owner)], ITERS + hedge_round, to).start()
         target[place(owner), :] = out[place(me), :]
 
@@ -718,6 +717,7 @@
             pltpu.SemaphoreType.DMA((2 * ITERS + 1,)),
             pltpu.SemaphoreType.DMA((2 * ITERS + 1,)),
             pltpu.SemaphoreType.REGULAR,
+            pltpu.SemaphoreType.REGULAR,
         ],
         compiler_params=pltpu.CompilerParams(
             collective_id=0, has_side_effects=True, vmem_limit_bytes=60 * 1024 * 1024
@@ -749,7 +749,7 @@
         tiles, demand, root_cost = args[0], args[4], args[5]
         tile = tiles.shape[5]
         cols, rows = root_cost.shape[0] // tile, demand.shape[1] // tile
-        if fits and tiles.shape[0] == 2 and tile == 128 and cols == rows == 2 * n_scen and cols % 8 == 0:
+        if fits and tiles.shape[0] == 2 and tile == 128 and cols == rows == 2 * n_scen and cols == 16:
             return fused_local(n_scen, *args)
         return local(*args)
 

time: 27.1 us -> 25.3 us (0.934)
  Pallas kernels: 26.3 us -> 24.5 us
    pallas_call x1, Pallas kernels: 24.7 us -> 22.9 us  [fused_local(): pl.pallas_call(functools.partial(fused, n_scen), out_shape=jax.ShapeDtype...]
where the time goes in v3:
time: 25.3 us; the launch traced here: 25.1 us
  Pallas kernels  24.5 us (97%)
  between operations  0.64 us (3%)
    pallas_call x1, Pallas kernels, fused_local(): pl.pallas_call(functools.partial(fused, n_scen), out_shape=jax.ShapeDtype...  22.9 us
    pallas_call x1, Pallas kernels, fused_local(): pl.pallas_call(unpack, out_shape=(col_shape,) * 6, in_specs=[pl.BlockSpec...  1.53 us

profile of v3, /device:TPU:0, one launch (start us, length us, event | category | flops | bytes accessed | tf_op | source)
XLA Modules:
  0.0 25.1 jit_solution(14227844492824568911)
XLA Ops:
  0.6 22.9 %shard_map.136.packed = f32[6,2,2048]{2,1,0:T(2,128)} custom-call(bf16[2,8,128,128]{3,2,1,0:T(8,128)(2,1)} %bitcast.3, s32[2,1,1,8]{3,2,1,0:T(1,128)} %row_index_in.1, s32[2,1,1,8]{3,2,1,0:T(1,128)} %col_index_in.1, s32[2]{0:T(128)} %bitcast.5, f32[2,2048]{1,0:T(2,128)} %demand_in.1, f32[16,128]{1,0:T(8,128)} %bitcast.4, f32[2,2048]{1,0:T(2,128)} %branch_cost_in.1, ...), custom_call_target="tpu_custom_call" | custom-call | tf_op jit(solution)/shard_map/pallas_call | solution.py:680
  23.6 1.5 %shard_map.137 = (f32[2,2048]{1,0:T(2,128)}, f32[2,2048]{1,0:T(2,128)}, f32[2,2048]{1,0:T(2,128)}, f32[2,2048]{1,0:T(2,128)}, f32[2,2048]{1,0:T(2,128)}, /*index=5*/f32[2,2048]{1,0:T(2,128)}) custom-call(f32[6,2,2048]{2,1,0:T(2,128)} %shard_map.136.packed), custom_call_target="tpu_custom_call" | custom-call | tf_op jit(solution)/shard_map/pallas_call | solution.py:736

commit v4 on v3

--- a/solution.py
+++ b/solution.py
@@ -216,9 +216,10 @@
     gather_in,
     reply_out,
     reply_in,
+    last_out,
+    last_in,
     branch_out,
     branch_in,
-    same_branch,
     early_out,
     early_in,
     late_out,
@@ -248,10 +249,12 @@
     total_scen = float(members)
     per_branch = float(members // BRANCHES)
 
-    owners = members // 2
+    owners = members // 4
     first_owner = members // 4
-    owner = me - first_owner
-    owns = jnp.logical_and(owner >= 0, owner < owners)
+    owner = chip - first_owner // 2
+    owns = jnp.logical_and(here == 1, jnp.logical_and(owner >= 0, owner < owners))
+    own_half = lax.rem(chip, 2)
+    own_ends = jnp.logical_and(owns, own_half == 1)
 
     def device_of(to):
         return {"scen": to // 2, "dep": lax.rem(to, 2)}
@@ -379,8 +382,8 @@
         for j in range(slots):
             flipped[half, j] = blocks[half, j].T
 
-    def place(index):
-        return pl.ds(pl.multiple_of(8 * index, 8), 8)
+    def place(index, rows):
+        return pl.ds(pl.multiple_of(rows * index, 8), rows)
 
     def group(source, target, at, to):
         return pltpu.make_async_remote_copy(
@@ -392,31 +395,22 @@
             device_id_type=MESH,
         )
 
-    def many(buffer, count, at):
-        part = buffer.at[pl.ds(0, 8 * count)]
+    def many(rows, at):
+        part = gather_in.at[0, pl.ds(0, rows)]
         return group(part, part, at, me + 1 - 2 * here)
 
-    def either(mine, others):
-        @pl.when(owns)
-        def _():
-            mine()
-
-        @pl.when(jnp.logical_not(owns))
-        def _():
-            others()
+    def either(test, mine, others):
+        pl.when(test)(mine)
+        pl.when(jnp.logical_not(test))(others)
 
     def in_order(x):
         own, far = x[:col_blocks], x[col_blocks:]
         return jnp.where(leads, own, far), jnp.where(leads, far, own)
 
-    def kind(k, count):
-        return pl.ds(k, count, stride=8)
-
     def to_owners(send):
-        half = owners // 2
-        home = me // half // 2 * half + lax.rem(me, half)
+        home = chip // owners * 2 + lax.rem(chip, 2)
         for k in reversed(range(owners)):
-            to = first_owner + jnp.bitwise_xor(home, k)
+            to = first_owner + 2 * jnp.bitwise_xor(home, k) + 1
             if k:
                 send(to)
             else:
@@ -437,18 +431,21 @@
     def gather_start(hedge_round, fleet, assign):
         buffer = gather_out.at[hedge_round]
         target = gather_in.at[hedge_round]
-        for k, value in enumerate(in_order(fleet) + in_order(assign)):
-            buffer[kind(2 * k, owners), :] = value[:owners]
-            buffer[kind(2 * k + 1, owners), :] = value[owners:]
+        fleets, assigns = in_order(fleet), in_order(assign)
+        for o in range(owners):
+            part = slice(o // 2 * 8, o // 2 * 8 + 8)
+            buffer[16 * o : 16 * o + 8, :] = fleets[o % 2][part]
+            buffer[16 * o + 8 : 16 * o + 16, :] = assigns[o % 2][part]
 
         def send(to):
-            group(buffer.at[place(to - first_owner)], target.at[place(me)], hedge_round, to).start()
+            source = buffer.at[place((to - first_owner) // 2, 16)]
+            group(source, target.at[place(me, 16)], hedge_round, to).start()
 
         to_owners(send)
 
         @pl.when(owns)
         def _():
-            target[place(me), :] = buffer[place(owner), :]
+            target[place(me, 16), :] = buffer[place(owner, 16), :]
 
     def reply_start(hedge_round):
         pl.when(owns)(functools.partial(reply, hedge_round))
@@ -457,66 +454,79 @@
         if hedge_round == 0:
             branch_wait(members - 1, lambda copy: copy.wait_recv())
             branch_in[me] = branch_out[...]
-            branches = jnp.concatenate([branch_in[k] for k in range(members)], axis=0)
-            lanes = lax.broadcasted_iota(jnp.int32, (members, tile), 1).astype(jnp.float32)
-            hot = (branches == lanes).astype(jnp.bfloat16)
-            same_branch[...] = dot_t(hot, hot)
-        many(gather_in.at[hedge_round], members - 1, hedge_round).wait_recv()
+        many(16 * (members - 1), hedge_round).wait_recv()
         buffer = gather_in.at[hedge_round]
-        parts = []
-        for k in range(4, 8):
-            value = buffer[kind(k, members), :]
-            high = value.astype(jnp.bfloat16)
-            rest = value - high.astype(jnp.float32)
-            middle = rest.astype(jnp.bfloat16)
-            low = (rest - middle.astype(jnp.float32)).astype(jnp.bfloat16)
-            parts += [high, middle, low]
-        sums = dot(same_branch[...].astype(jnp.bfloat16), jnp.concatenate(parts, axis=1))
-        pieces = [sums[:, i * tile : (i + 1) * tile] for i in range(12)]
-        means = [
-            ((pieces[3 * k + 2] + pieces[3 * k + 1]) + pieces[3 * k]) / per_branch for k in range(4)
-        ]
-        fleets = [
-            jnp.broadcast_to(
-                jnp.sum(buffer[kind(k, members), :], axis=0, keepdims=True) / total_scen,
-                (members, tile),
-            )
-            for k in range(4)
-        ]
+        fleet_sum = buffer[0:8, :]
+        for k in range(1, members):
+            fleet_sum = fleet_sum + buffer[16 * k : 16 * k + 8, :]
+        fleet_means = fleet_sum / total_scen
+        branches = [jnp.broadcast_to(branch_in[k], (8, tile)) for k in range(members)]
+        assigns = [buffer[16 * k + 8 : 16 * k + 16, :] for k in range(members)]
+        sums = list(assigns)
+        for k in range(members):
+            for m in range(k + 1, members):
+                same = branches[k] == branches[m]
+                sums[k] = sums[k] + jnp.where(same, assigns[m], 0.0)
+                sums[m] = sums[m] + jnp.where(same, assigns[k], 0.0)
+        means = [x / per_branch for x in sums]
         if hedge_round < ITERS - 1:
-            values = fleets + means
+            for k in range(members):
+                reply_out[16 * k : 16 * k + 8, :] = fleet_means
+                reply_out[16 * k + 8 : 16 * k + 16, :] = means[k]
+            for k in far_first(members):
+                to = jnp.bitwise_xor(me, k)
+                source, target = reply_out.at[place(to, 16)], reply_in.at[place(owner, 16)]
+                group(source, target, ITERS + hedge_round, to).start()
+            reply_in[place(owner, 16), :] = reply_out[place(me, 16), :]
         else:
-            even = lax.rem(lax.broadcasted_iota(jnp.int32, (members, tile), 0), 2) == 0
-            down = [jnp.concatenate([x[-1:], x[:-1]], axis=0) for x in means[2:]]
-            up = [jnp.concatenate([x[1:], x[:1]], axis=0) for x in means[:2]]
-            values = [jnp.where(even, fleets[k], fleets[2 + k]) for k in range(2)]
-            values += [jnp.where(even, means[k], down[k]) for k in range(2)]
-            values += [jnp.where(even, up[k], means[2 + k]) for k in range(2)]
-            values += [jnp.zeros((members, tile), jnp.float32)] * 2
-        out, target = reply_out.at[hedge_round], reply_in.at[hedge_round]
-        for k, value in enumerate(values):
-            out[kind(k, members), :] = value
-        quarter = members // 4
+            for k in range(n_scen):
+                last_out[24 * k : 24 * k + 8, :] = fleet_means
+                last_out[24 * k + 8 : 24 * k + 16, :] = means[2 * k]
+                last_out[24 * k + 16 : 24 * k + 24, :] = means[2 * k + 1]
+            target = last_in.at[place(owner // 2, 24)]
+
+            def send(k):
+                there = jnp.bitwise_xor(chip, k)
+                source = last_out.at[place(there, 24)]
+                group(source, target, ITERS + hedge_round, 2 * there + own_half).start()
+
+            for k in far_first(n_scen):
+                send(k)
+
+            @pl.when(own_half == 0)
+            def _():
+                send(0)
+
+            @pl.when(own_half == 1)
+            def _():
+                last_in[place(owner // 2, 24), :] = last_out[place(chip, 24), :]
+
+    def far_first(count):
+        quarter = count // 4
         near_last = [2, 3, 1, 0]
-        for k in sorted(range(1, members), key=lambda k: (near_last.index(k // quarter), -k)):
-            to = jnp.bitwise_xor(me, k)
-            group(out.at[place(to)], target.at[place(owner)], ITERS + hedge_round, to).start()
-        target[place(owner), :] = out[place(me), :]
+        return sorted(range(1, count), key=lambda k: (near_last.index(k // quarter), -k))
 
     def reply_wait(hedge_round):
-        buffer, at = reply_in.at[hedge_round], ITERS + hedge_round
-        either(
-            lambda: many(buffer, owners - 1, at).wait_recv(),
-            lambda: many(buffer, owners, at).wait_recv(),
-        )
-
-    def reply_half(hedge_round, k):
-        back = reply_in.at[hedge_round]
-        return jnp.concatenate([back[kind(k, owners), :], back[kind(k + 1, owners), :]], axis=0)
-
-    def reply_all(hedge_round, k):
-        halves = jnp.concatenate([reply_half(hedge_round, k), reply_half(hedge_round, k + 2)], axis=0)
-        return jnp.concatenate(in_order(halves), axis=0)
+        at = ITERS + hedge_round
+        if hedge_round < ITERS - 1:
+            either(
+                owns,
+                lambda: many(16 * (owners - 1), at).wait_recv(),
+                lambda: many(16 * owners, at).wait_recv(),
+            )
+        else:
+            either(
+                own_ends,
+                lambda: many(24 * (owners // 2 - 1), at).wait_recv(),
+                lambda: many(24 * (owners // 2), at).wait_recv(),
+            )
+
+    def reply_all(k):
+        halves = [reply_in[16 * o + k : 16 * o + k + 8, :] for o in (0, 2, 1, 3)]
+        return jnp.concatenate(in_order(jnp.concatenate(halves, axis=0)), axis=0)
+
+    def last_half(k):
+        return jnp.concatenate([last_in[k : k + 8, :], last_in[24 + k : 32 + k, :]], axis=0)
 
     def group_enter():
         @pl.when(here == 1)
@@ -588,8 +598,8 @@
                 late_copy.start()
             if waits:
                 reply_wait(hedge_round - 1)
-                fleet_mean = reply_all(hedge_round - 1, 0)
-                assign_mean = reply_all(hedge_round - 1, 4)
+                fleet_mean = reply_all(0)
+                assign_mean = reply_all(8)
                 fleet_price = fleet_price + penalty * (fleet - fleet_mean)
                 assign_price = assign_price + penalty * (assign - assign_mean)
                 fleet_new, assign_new = plans()
@@ -625,8 +635,7 @@
     put_out(2, dispatch[:col_blocks], late_in[0])
     put_out(3, cover, late_in[1])
     reply_wait(ITERS - 1)
-    last_fleet = reply_half(ITERS - 1, 0)
-    even_mean, odd_mean = reply_half(ITERS - 1, 2), reply_half(ITERS - 1, 4)
+    last_fleet, even_mean, odd_mean = last_half(0), last_half(8), last_half(16)
     own_mean = jnp.where(here == 0, even_mean, odd_mean)
     far_mean = jnp.where(here == 0, odd_mean, even_mean)
     put_out(
@@ -643,15 +652,20 @@
     def sent_by_owner():
         branch_wait(owners - 1, lambda copy: copy.wait_send())
         for r in range(ITERS):
-            many(gather_in.at[r], owners - 1, r).wait_send()
-            many(gather_in.at[r], members - 1, ITERS + r).wait_send()
+            many(16 * (owners - 1), r).wait_send()
+        many(16 * (members - 1), ITERS).wait_send()
+        either(
+            own_ends,
+            lambda: many(24 * (n_scen - 1), 2 * ITERS - 1).wait_send(),
+            lambda: many(24 * n_scen, 2 * ITERS - 1).wait_send(),
+        )
 
     def sent_by_others():
         branch_wait(owners, lambda copy: copy.wait_send())
         for r in range(ITERS):
-            many(gather_in.at[r], owners, r).wait_send()
-
-    either(sent_by_owner, sent_by_others)
+            many(16 * owners, r).wait_send()
+
+    either(owns, sent_by_owner, sent_by_others)
 
 
 def unpack(packed, *outs):
@@ -700,12 +714,13 @@
             pltpu.VMEM((rows, tile), f32),
             pltpu.VMEM((2 * cols, tile), f32),
             pltpu.VMEM((ITERS, 4 * members, tile), f32),
-            pltpu.VMEM((ITERS, 8 * members, tile), f32),
-            pltpu.VMEM((ITERS, 8 * members, tile), f32),
-            pltpu.VMEM((ITERS, 4 * members, tile), f32),
+            pltpu.VMEM((ITERS, 16 * members, tile), f32),
+            pltpu.VMEM((16 * members, tile), f32),
+            pltpu.VMEM((4 * members, tile), f32),
+            pltpu.VMEM((24 * n_scen, tile), f32),
+            pltpu.VMEM((48, tile), f32),
             pltpu.VMEM((1, tile), f32),
             pltpu.VMEM((members, 1, tile), f32),
-            pltpu.VMEM((members, members), f32),
             pltpu.VMEM((4, cols, tile), f32),
             pltpu.VMEM((4, cols, tile), f32),
             pltpu.VMEM((2, cols, tile), f32),

time: 25.3 us -> 23.6 us (0.933)
  Pallas kernels: 24.5 us -> 22.8 us
    pallas_call x1, Pallas kernels: 22.9 us -> 21.2 us  [fused_local(): pl.pallas_call(functools.partial(fused, n_scen), out_shape=jax.ShapeDtype...]
where the time goes in v4:
time: 23.6 us; the launch traced here: 23.4 us
  Pallas kernels  22.8 us (97%)
  between operations  0.64 us (3%)
    pallas_call x1, Pallas kernels, fused_local(): pl.pallas_call(functools.partial(fused, n_scen), out_shape=jax.ShapeDtype...  21.2 us
    pallas_call x1, Pallas kernels, fused_local(): pl.pallas_call(unpack, out_shape=(col_shape,) * 6, in_specs=[pl.BlockSpec...  1.53 us

profile of v4, /device:TPU:0, one launch (start us, length us, event | category | flops | bytes accessed | tf_op | source)
XLA Modules:
  0.0 23.4 jit_solution(986803690802464665)
XLA Ops:
  0.6 21.2 %shard_map.136.packed = f32[6,2,2048]{2,1,0:T(2,128)} custom-call(bf16[2,8,128,128]{3,2,1,0:T(8,128)(2,1)} %bitcast.3, s32[2,1,1,8]{3,2,1,0:T(1,128)} %row_index_in.1, s32[2,1,1,8]{3,2,1,0:T(1,128)} %col_index_in.1, s32[2]{0:T(128)} %bitcast.5, f32[2,2048]{1,0:T(2,128)} %demand_in.1, f32[16,128]{1,0:T(8,128)} %bitcast.4, f32[2,2048]{1,0:T(2,128)} %branch_cost_in.1, ...), custom_call_target="tpu_custom_call" | custom-call | tf_op jit(solution)/shard_map/pallas_call | solution.py:694
  21.9 1.5 %shard_map.137 = (f32[2,2048]{1,0:T(2,128)}, f32[2,2048]{1,0:T(2,128)}, f32[2,2048]{1,0:T(2,128)}, f32[2,2048]{1,0:T(2,128)}, f32[2,2048]{1,0:T(2,128)}, /*index=5*/f32[2,2048]{1,0:T(2,128)}) custom-call(f32[6,2,2048]{2,1,0:T(2,128)} %shard_map.136.packed), custom_call_target="tpu_custom_call" | custom-call | tf_op jit(solution)/shard_map/pallas_call | solution.py:751

commit v5 on v4

--- a/solution.py
+++ b/solution.py
@@ -253,8 +253,9 @@
     first_owner = members // 4
     owner = chip - first_owner // 2
     owns = jnp.logical_and(here == 1, jnp.logical_and(owner >= 0, owner < owners))
-    own_half = lax.rem(chip, 2)
-    own_ends = jnp.logical_and(owns, own_half == 1)
+    plane = lax.rem(chip, 2)
+    own_half = owner // 2
+    own_ends = jnp.logical_and(owns, owner >= 2)
 
     def device_of(to):
         return {"scen": to // 2, "dep": lax.rem(to, 2)}
@@ -432,20 +433,19 @@
         buffer = gather_out.at[hedge_round]
         target = gather_in.at[hedge_round]
         fleets, assigns = in_order(fleet), in_order(assign)
-        for o in range(owners):
-            part = slice(o // 2 * 8, o // 2 * 8 + 8)
-            buffer[16 * o : 16 * o + 8, :] = fleets[o % 2][part]
-            buffer[16 * o + 8 : 16 * o + 16, :] = assigns[o % 2][part]
+        for half in range(2):
+            buffer[32 * half : 32 * half + 16, :] = fleets[half]
+            buffer[32 * half + 16 : 32 * half + 32, :] = assigns[half]
 
         def send(to):
-            source = buffer.at[place((to - first_owner) // 2, 16)]
-            group(source, target.at[place(me, 16)], hedge_round, to).start()
+            source = buffer.at[place((to - first_owner) // 4, 32)]
+            group(source, target.at[place(me, 32)], hedge_round, to).start()
 
         to_owners(send)
 
         @pl.when(owns)
         def _():
-            target[place(me, 16), :] = buffer[place(owner, 16), :]
+            target[place(me, 32), :] = buffer[place(own_half, 32), :]
 
     def reply_start(hedge_round):
         pl.when(owns)(functools.partial(reply, hedge_round))
@@ -454,43 +454,45 @@
         if hedge_round == 0:
             branch_wait(members - 1, lambda copy: copy.wait_recv())
             branch_in[me] = branch_out[...]
-        many(16 * (members - 1), hedge_round).wait_recv()
+        many(32 * (members - 1), hedge_round).wait_recv()
         buffer = gather_in.at[hedge_round]
-        fleet_sum = buffer[0:8, :]
-        for k in range(1, members):
-            fleet_sum = fleet_sum + buffer[16 * k : 16 * k + 8, :]
-        fleet_means = fleet_sum / total_scen
         branches = [jnp.broadcast_to(branch_in[k], (8, tile)) for k in range(members)]
-        assigns = [buffer[16 * k + 8 : 16 * k + 16, :] for k in range(members)]
-        sums = list(assigns)
-        for k in range(members):
-            for m in range(k + 1, members):
-                same = branches[k] == branches[m]
-                sums[k] = sums[k] + jnp.where(same, assigns[m], 0.0)
-                sums[m] = sums[m] + jnp.where(same, assigns[k], 0.0)
-        means = [x / per_branch for x in sums]
-        if hedge_round < ITERS - 1:
+        near = plane == 0
+        last = hedge_round == ITERS - 1
+        for part in (0, 8):
+            fleet_sum = buffer[part : part + 8, :]
+            for k in range(1, members):
+                fleet_sum = fleet_sum + buffer[32 * k + part : 32 * k + part + 8, :]
+            fleet_means = fleet_sum / total_scen
+            assigns = [buffer[32 * k + 16 + part : 32 * k + 24 + part, :] for k in range(members)]
+            sums = list(assigns)
             for k in range(members):
-                reply_out[16 * k : 16 * k + 8, :] = fleet_means
-                reply_out[16 * k + 8 : 16 * k + 16, :] = means[k]
-            for k in far_first(members):
-                to = jnp.bitwise_xor(me, k)
-                source, target = reply_out.at[place(to, 16)], reply_in.at[place(owner, 16)]
-                group(source, target, ITERS + hedge_round, to).start()
-            reply_in[place(owner, 16), :] = reply_out[place(me, 16), :]
-        else:
-            for k in range(n_scen):
-                last_out[24 * k : 24 * k + 8, :] = fleet_means
-                last_out[24 * k + 8 : 24 * k + 16, :] = means[2 * k]
-                last_out[24 * k + 16 : 24 * k + 24, :] = means[2 * k + 1]
-            target = last_in.at[place(owner // 2, 24)]
-
+                for m in range(k + 1, members):
+                    same = branches[k] == branches[m]
+                    sums[k] = sums[k] + jnp.where(same, assigns[m], 0.0)
+                    sums[m] = sums[m] + jnp.where(same, assigns[k], 0.0)
+            for z in range(n_scen // 2):
+                pair_means = [
+                    jnp.where(near, sums[4 * z + c], sums[4 * z + 2 + c]) / per_branch for c in range(2)
+                ]
+                if last:
+                    at = 48 * z + part
+                    last_out[at : at + 8, :] = fleet_means
+                    last_out[at + 16 : at + 24, :] = pair_means[0]
+                    last_out[at + 32 : at + 40, :] = pair_means[1]
+                else:
+                    for c in range(2):
+                        at = 32 * (2 * z + c) + part
+                        reply_out[at : at + 8, :] = fleet_means
+                        reply_out[at + 16 : at + 24, :] = pair_means[c]
+        if last:
             def send(k):
-                there = jnp.bitwise_xor(chip, k)
-                source = last_out.at[place(there, 24)]
-                group(source, target, ITERS + hedge_round, 2 * there + own_half).start()
-
-            for k in far_first(n_scen):
+                there = jnp.bitwise_xor(chip // 2, k)
+                source = last_out.at[place(there, 48)]
+                to = 4 * there + 2 * plane + own_half
+                group(source, last_in, ITERS + hedge_round, to).start()
+
+            for k in (2, 3, 1):
                 send(k)
 
             @pl.when(own_half == 0)
@@ -499,34 +501,29 @@
 
             @pl.when(own_half == 1)
             def _():
-                last_in[place(owner // 2, 24), :] = last_out[place(chip, 24), :]
-
-    def far_first(count):
-        quarter = count // 4
-        near_last = [2, 3, 1, 0]
-        return sorted(range(1, count), key=lambda k: (near_last.index(k // quarter), -k))
+                last_in[...] = last_out[place(chip // 2, 48), :]
+        else:
+            slot = chip // 2 * 2 + 1
+            for k in (5, 4, 7, 6, 3, 2, 1):
+                there = jnp.bitwise_xor(slot, k)
+                to = there // 2 * 4 + 2 * plane + lax.rem(there, 2)
+                source, target = reply_out.at[place(there, 32)], reply_in.at[place(own_half, 32)]
+                group(source, target, ITERS + hedge_round, to).start()
+            reply_in[place(own_half, 32), :] = reply_out[place(slot, 32), :]
 
     def reply_wait(hedge_round):
         at = ITERS + hedge_round
         if hedge_round < ITERS - 1:
-            either(
-                owns,
-                lambda: many(16 * (owners - 1), at).wait_recv(),
-                lambda: many(16 * owners, at).wait_recv(),
-            )
+            either(owns, lambda: many(32, at).wait_recv(), lambda: many(64, at).wait_recv())
         else:
-            either(
-                own_ends,
-                lambda: many(24 * (owners // 2 - 1), at).wait_recv(),
-                lambda: many(24 * (owners // 2), at).wait_recv(),
-            )
+            pl.when(jnp.logical_not(own_ends))(lambda: many(48, at).wait_recv())
 
     def reply_all(k):
-        halves = [reply_in[16 * o + k : 16 * o + k + 8, :] for o in (0, 2, 1, 3)]
+        halves = [reply_in[k : k + 16, :], reply_in[32 + k : 48 + k, :]]
         return jnp.concatenate(in_order(jnp.concatenate(halves, axis=0)), axis=0)
 
     def last_half(k):
-        return jnp.concatenate([last_in[k : k + 8, :], last_in[24 + k : 32 + k, :]], axis=0)
+        return last_in[k : k + 16, :]
 
     def group_enter():
         @pl.when(here == 1)
@@ -599,7 +596,7 @@
             if waits:
                 reply_wait(hedge_round - 1)
                 fleet_mean = reply_all(0)
-                assign_mean = reply_all(8)
+                assign_mean = reply_all(16)
                 fleet_price = fleet_price + penalty * (fleet - fleet_mean)
                 assign_price = assign_price + penalty * (assign - assign_mean)
                 fleet_new, assign_new = plans()
@@ -611,10 +608,10 @@
                 primal_moves = total(
                     (fleet_new - fleet) ** 2 + (assign_new - assign) ** 2 + (dispatch_new - dispatch) ** 2
                 )
-                pair_moves = total((assign_dual_new - assign_dual) ** 2 + (fleet_dual_new - fleet_dual) ** 2)
-                cover_moves = total((cover_new - cover) ** 2)
+                pair_moves = (assign_dual_new - assign_dual) ** 2 + (fleet_dual_new - fleet_dual) ** 2
+                dual_moves = total(pair_moves[:row_blocks] + pair_moves[row_blocks:] + (cover_new - cover) ** 2)
                 primal_rate = primal_moves / (3.0 * col_total)
-                dual_rate = (cover_moves + pair_moves) / (lane_total + 2.0 * col_total)
+                dual_rate = dual_moves / (lane_total + 2.0 * col_total)
                 target = jnp.sqrt((primal_rate + epsilon) / (dual_rate + epsilon))
                 ratio = jnp.sqrt(ratio * target)
                 fleet_dual, assign_dual = fleet_dual_new, assign_dual_new
@@ -635,7 +632,7 @@
     put_out(2, dispatch[:col_blocks], late_in[0])
     put_out(3, cover, late_in[1])
     reply_wait(ITERS - 1)
-    last_fleet, even_mean, odd_mean = last_half(0), last_half(8), last_half(16)
+    last_fleet, even_mean, odd_mean = last_half(0), last_half(16), last_half(32)
     own_mean = jnp.where(here == 0, even_mean, odd_mean)
     far_mean = jnp.where(here == 0, odd_mean, even_mean)
     put_out(
@@ -652,18 +649,18 @@
     def sent_by_owner():
         branch_wait(owners - 1, lambda copy: copy.wait_send())
         for r in range(ITERS):
-            many(16 * (owners - 1), r).wait_send()
-        many(16 * (members - 1), ITERS).wait_send()
+            many(32 * (owners - 1), r).wait_send()
+        many(32 * (n_scen - 1), ITERS).wait_send()
         either(
             own_ends,
-            lambda: many(24 * (n_scen - 1), 2 * ITERS - 1).wait_send(),
-            lambda: many(24 * n_scen, 2 * ITERS - 1).wait_send(),
+            lambda: many(48 * (n_scen // 2 - 1), 2 * ITERS - 1).wait_send(),
+            lambda: many(48 * (n_scen // 2), 2 * ITERS - 1).wait_send(),
         )
 
     def sent_by_others():
         branch_wait(owners, lambda copy: copy.wait_send())
         for r in range(ITERS):
-            many(16 * owners, r).wait_send()
+            many(32 * owners, r).wait_send()
 
     either(owns, sent_by_owner, sent_by_others)
 
@@ -714,7 +711,7 @@
             pltpu.VMEM((rows, tile), f32),
             pltpu.VMEM((2 * cols, tile), f32),
             pltpu.VMEM((ITERS, 4 * members, tile), f32),
-            pltpu.VMEM((ITERS, 16 * members, tile), f32),
+            pltpu.VMEM((ITERS, 32 * members, tile), f32),
             pltpu.VMEM((16 * members, tile), f32),
             pltpu.VMEM((4 * members, tile), f32),
             pltpu.VMEM((24 * n_scen, tile), f32),

time: 23.6 us -> 23.3 us (0.987)
  Pallas kernels: 22.8 us -> 22.5 us
    pallas_call x1, Pallas kernels: 21.2 us -> 21 us  [fused_local(): pl.pallas_call(functools.partial(fused, n_scen), out_shape=jax.ShapeDtype...]
where the time goes in v5:
time: 23.3 us; the launch traced here: 23.1 us
  Pallas kernels  22.5 us (97%)
  between operations  0.64 us (3%)
    pallas_call x1, Pallas kernels, fused_local(): pl.pallas_call(functools.partial(fused, n_scen), out_shape=jax.ShapeDtype...  21 us
    pallas_call x1, Pallas kernels, fused_local(): pl.pallas_call(unpack, out_shape=(col_shape,) * 6, in_specs=[pl.BlockSpec...  1.53 us

profile of v5, /device:TPU:0, one launch (start us, length us, event | category | flops | bytes accessed | tf_op | source)
XLA Modules:
  0.0 23.1 jit_solution(7749275129017139423)
XLA Ops:
  0.6 21.0 %shard_map.136.packed = f32[6,2,2048]{2,1,0:T(2,128)} custom-call(bf16[2,8,128,128]{3,2,1,0:T(8,128)(2,1)} %bitcast.3, s32[2,1,1,8]{3,2,1,0:T(1,128)} %row_index_in.1, s32[2,1,1,8]{3,2,1,0:T(1,128)} %col_index_in.1, s32[2]{0:T(128)} %bitcast.5, f32[2,2048]{1,0:T(2,128)} %demand_in.1, f32[16,128]{1,0:T(8,128)} %bitcast.4, f32[2,2048]{1,0:T(2,128)} %branch_cost_in.1, ...), custom_call_target="tpu_custom_call" | custom-call | tf_op jit(solution)/shard_map/pallas_call | solution.py:691
  21.6 1.5 %shard_map.137 = (f32[2,2048]{1,0:T(2,128)}, f32[2,2048]{1,0:T(2,128)}, f32[2,2048]{1,0:T(2,128)}, f32[2,2048]{1,0:T(2,128)}, f32[2,2048]{1,0:T(2,128)}, /*index=5*/f32[2,2048]{1,0:T(2,128)}) custom-call(f32[6,2,2048]{2,1,0:T(2,128)} %shard_map.136.packed), custom_call_target="tpu_custom_call" | custom-call | tf_op jit(solution)/shard_map/pallas_call | solution.py:748

commit v6 on v5

--- a/solution.py
+++ b/solution.py
@@ -572,7 +572,7 @@
 
             if not waits:
                 fleet_new, assign_new = plans()
-            if hedge_round == 0 and inner_step == STEPS - 2:
+            if hedge_round == 0 and inner_step == STEPS - 1:
                 group_enter()
                 branch_start()
             if ends:

time: 23.3 us -> 23.4 us (level)
  no operation moved by 1% of the time
where the time goes in v6:
time: 23.4 us; the launch traced here: 23.2 us
  Pallas kernels  22.5 us (96%)
  between operations  0.64 us (3%)
    pallas_call x1, Pallas kernels, fused_local(): pl.pallas_call(functools.partial(fused, n_scen), out_shape=jax.ShapeDtype...  21 us
    pallas_call x1, Pallas kernels, fused_local(): pl.pallas_call(unpack, out_shape=(col_shape,) * 6, in_specs=[pl.BlockSpec...  1.53 us

profile of v6, /device:TPU:0, one launch (start us, length us, event | category | flops | bytes accessed | tf_op | source)
XLA Modules:
  0.0 23.2 jit_solution(11603620774074718283)
XLA Ops:
  0.6 21.0 %shard_map.136.packed = f32[6,2,2048]{2,1,0:T(2,128)} custom-call(bf16[2,8,128,128]{3,2,1,0:T(8,128)(2,1)} %bitcast.3, s32[2,1,1,8]{3,2,1,0:T(1,128)} %row_index_in.1, s32[2,1,1,8]{3,2,1,0:T(1,128)} %col_index_in.1, s32[2]{0:T(128)} %bitcast.5, f32[2,2048]{1,0:T(2,128)} %demand_in.1, f32[16,128]{1,0:T(8,128)} %bitcast.4, f32[2,2048]{1,0:T(2,128)} %branch_cost_in.1, ...), custom_call_target="tpu_custom_call" | custom-call | tf_op jit(solution)/shard_map/pallas_call | solution.py:691
  21.6 1.5 %shard_map.137 = (f32[2,2048]{1,0:T(2,128)}, f32[2,2048]{1,0:T(2,128)}, f32[2,2048]{1,0:T(2,128)}, f32[2,2048]{1,0:T(2,128)}, f32[2,2048]{1,0:T(2,128)}, /*index=5*/f32[2,2048]{1,0:T(2,128)}) custom-call(f32[6,2,2048]{2,1,0:T(2,128)} %shard_map.136.packed), custom_call_target="tpu_custom_call" | custom-call | tf_op jit(solution)/shard_map/pallas_call | solution.py:748
